TPU v7x, 512 devices: a whole 4x8x8 slice. The times are simulated.
512 devices in a mesh: row: 16 (over y_lo, x, core), col: 32 (over z, y_hi).
Axes of the slice: x: 4, y: 8 (y_hi: 4, y_lo: 2; y = y_hi * 2 + y_lo), z: 8, core: 2. Of those that a mesh axis runs over, the one named last changes fastest.
Arguments:
- query_tokens: bfloat16 [512, 192, 1024], P('row', 'col'), may hold values from -11 to 11
- key_tokens: bfloat16 [512, 192, 1024], P('row', 'col'), may hold values from -6 to 6
- value_tokens: bfloat16 [512, 192, 1024], P('row', 'col'), may hold values from -6 to 6
- merge_sizes: int32 [512, 192], P('row', 'col'), may hold values from 1 to 16
- w_out: bfloat16 [1024, 1024], P(None, 'row'), may hold values from -0.1875 to 0.1875
Outputs:
- mixed: bfloat16 [512, 192, 1024], P('row', 'col')
All inputs are finite; a program needn't handle non-finite values.
Results may differ from a plain program's by a relative error of at most 0.0085.
Values may be sent and summed in bfloat16 or wider, within the bound.
No kernel may reach another device: no remote copies, remote signals or barrier semaphores. Data moves between devices by JAX's collectives and lax.ppermute only.
A program may use at most 64 MiB of HBM per device.

v0:
```python
import jax
import jax.numpy as jnp
from jax import lax
from jax.sharding import PartitionSpec as P

HEADS = 16
HEAD = 64


NEG_START = -1e30


def on_device(query_tokens, key_tokens, value_tokens, merge_sizes, w_out):
    row_count, col_count, model_width = query_tokens.shape
    half_heads = HEADS // 2
    half_width = half_heads * HEAD
    score_scale = HEAD ** (-0.5)
    key_bias = jnp.log(merge_sizes.astype(jnp.float32)).astype(jnp.bfloat16)
    column_query = query_tokens[:, :, :half_width].reshape(row_count, col_count, half_heads, HEAD)
    column_keys = key_tokens[:, :, :half_width].reshape(row_count, col_count, half_heads, HEAD)
    column_values = value_tokens[:, :, :half_width].reshape(row_count, col_count, half_heads, HEAD)
    running = jnp.full((col_count, half_heads, row_count), NEG_START, jnp.float32)
    key_piece = lax.all_gather(column_keys, "row", axis=0, tiled=True)
    value_piece = lax.all_gather(column_values, "row", axis=0, tiled=True)
    bias_piece = lax.all_gather(key_bias, "row", axis=0, tiled=True)
    scores = (
        jnp.einsum("rchd,kchd->chrk", column_query, key_piece, preferred_element_type=jnp.float32)
        * score_scale
    )
    scores = scores + jnp.transpose(bias_piece).astype(jnp.float32)[:, None, None, :]
    updated = jnp.maximum(running, jnp.max(scores, axis=-1))
    weights = jnp.exp(scores - updated[..., None])
    summed = jnp.sum(weights, axis=-1)
    contribution = jnp.einsum(
        "chrk,kchd->chrd",
        weights.astype(jnp.bfloat16),
        value_piece,
        preferred_element_type=jnp.float32,
    )
    column_out = (contribution / summed[..., None]).astype(jnp.bfloat16)
    column_out = jnp.transpose(column_out, (2, 0, 1, 3)).reshape(row_count, col_count, half_width)
    moved_rows = (
        lax.all_to_all(
            query_tokens[:, :, half_width:], "col", split_axis=0, concat_axis=1, tiled=True
        ),
        lax.all_to_all(
            key_tokens[:, :, half_width:], "col", split_axis=0, concat_axis=1, tiled=True
        ),
        lax.all_to_all(
            value_tokens[:, :, half_width:], "col", split_axis=0, concat_axis=1, tiled=True
        ),
        lax.all_to_all(key_bias, "col", split_axis=0, concat_axis=1, tiled=True),
    )
    line_rows = moved_rows[0].shape[0]
    line_length = moved_rows[0].shape[1]
    row_query = moved_rows[0].reshape(line_rows, line_length, half_heads, HEAD)
    row_keys = moved_rows[1].reshape(line_rows, line_length, half_heads, HEAD)
    row_values = moved_rows[2].reshape(line_rows, line_length, half_heads, HEAD)
    row_scores = (
        jnp.einsum("rchd,rkhd->rhck", row_query, row_keys, preferred_element_type=jnp.float32)
        * score_scale
    )
    row_scores = row_scores + moved_rows[3].astype(jnp.float32)[:, None, None, :]
    row_highest = jnp.max(row_scores, axis=-1, keepdims=True)
    row_weights = jnp.exp(row_scores - row_highest)
    row_summed = jnp.sum(row_weights, axis=-1)
    row_combined = jnp.einsum(
        "rhck,rkhd->rchd",
        row_weights.astype(jnp.bfloat16),
        row_values,
        preferred_element_type=jnp.float32,
    )
    row_combined = row_combined / jnp.transpose(row_summed, (0, 2, 1))[..., None]
    local_rows = row_combined.astype(jnp.bfloat16).reshape(line_rows, line_length, half_width)
    row_out = lax.all_to_all(local_rows, "col", split_axis=1, concat_axis=0, tiled=True)
    joined = jnp.concatenate([column_out, row_out], axis=-1).reshape(
        row_count * col_count, model_width
    )
    projected = jnp.dot(
        joined, lax.all_gather(w_out, "row", axis=1, tiled=True), preferred_element_type=jnp.float32
    )
    return projected.astype(jnp.bfloat16).reshape(row_count, col_count, model_width)


def solution(mesh):
    return jax.shard_map(
        on_device,
        mesh=mesh,
        in_specs=(
            P("row", "col", None),
            P("row", "col", None),
            P("row", "col", None),
            P("row", "col"),
            P(None, "row"),
        ),
        out_specs=P("row", "col", None),
        check_vma=False,
    )
```

profile of v0, /device:TPU:1, one launch (start us, length us, event | category | flops | bytes accessed | tf_op | source)
XLA Modules:
  0.0 178.1 jit_solution(18168808942532495227)
XLA Ops:
  6.5 1.1 fusion.36
  7.9 0.8 copy.56
  8.8 1.1 fusion.37
  10.1 0.8 copy.59
  11.6 16.5 %all-to-all-start.2 = ((bf16[32,1,6]{2,1,0:T(2,128)(2,1)}), bf16[32,1,6]{2,1,0:T(2,128)(2,1)S(1)}, u32[]{:S(2)}, u32[]{:S(2)}) async-start(bf16[32,1,6]{2,1,0:T(2,128)(2,1)} %copy.65), calls=%async_computation.2 | async-start | bytes 32768 | tf_op jit(solution)/shard_map/all_to_all | solution.py:52
  29.0 0.8 copy.74
  29.8 9.4 %all-to-all-done.2 = bf16[32,1,6]{2,1,0:T(2,128)(2,1)S(1)} async-done(((bf16[32,1,6]{2,1,0:T(2,128)(2,1)}), bf16[32,1,6]{2,1,0:T(2,128)(2,1)S(1)}, u32[]{:S(2)}, u32[]{:S(2)}) %all-to-all-start.2) | async-done | bytes 416 | tf_op jit(solution)/shard_map/all_to_all | solution.py:52
  39.2 3.9 %all-to-all-start = ((bf16[32,6,512]{2,1,0:T(8,128)(2,1)}), bf16[32,6,512]{2,1,0:T(8,128)(2,1)S(1)}, u32[]{:S(2)}, u32[]{:S(2)}) async-start(bf16[32,6,512]{2,1,0:T(8,128)(2,1)} %copy.74), calls=%async_computation | async-start | bytes 524288 | tf_op jit(solution)/shard_map/all_to_all | solution.py:43
  43.0 0.8 copy.75
  43.9 14.8 %all-to-all-done = bf16[32,6,512]{2,1,0:T(8,128)(2,1)S(1)} async-done(((bf16[32,6,512]{2,1,0:T(8,128)(2,1)}), bf16[32,6,512]{2,1,0:T(8,128)(2,1)S(1)}, u32[]{:S(2)}, u32[]{:S(2)}) %all-to-all-start) | async-done | bytes 196640 | tf_op jit(solution)/shard_map/all_to_all | solution.py:43
  58.7 4.6 %all-to-all-start.1 = ((bf16[32,6,512]{2,1,0:T(8,128)(2,1)}), bf16[32,6,512]{2,1,0:T(8,128)(2,1)S(1)}, u32[]{:S(2)}, u32[]{:S(2)}) async-start(bf16[32,6,512]{2,1,0:T(8,128)(2,1)} %copy.75), calls=%async_computation.1 | async-start | bytes 524288 | tf_op jit(solution)/shard_map/all_to_all | solution.py:46
  63.3 0.8 copy.73
  64.1 14.1 %all-to-all-done.1 = bf16[32,6,512]{2,1,0:T(8,128)(2,1)S(1)} async-done(((bf16[32,6,512]{2,1,0:T(8,128)(2,1)}), bf16[32,6,512]{2,1,0:T(8,128)(2,1)S(1)}, u32[]{:S(2)}, u32[]{:S(2)}) %all-to-all-start.1) | async-done | bytes 196640 | tf_op jit(solution)/shard_map/all_to_all | solution.py:46
  78.3 5.2 %all-to-all-start.3 = ((bf16[32,6,512]{2,1,0:T(8,128)(2,1)}), bf16[32,6,512]{2,1,0:T(8,128)(2,1)S(1)}, u32[]{:S(2)}, u32[]{:S(2)}) async-start(bf16[32,6,512]{2,1,0:T(8,128)(2,1)} %copy.73), calls=%async_computation.3 | async-start | bytes 524288 | tf_op jit(solution)/shard_map/all_to_all | solution.py:49
  84.1 11.2 %all-to-all-done.3 = bf16[32,6,512]{2,1,0:T(8,128)(2,1)S(1)} async-done(((bf16[32,6,512]{2,1,0:T(8,128)(2,1)}), bf16[32,6,512]{2,1,0:T(8,128)(2,1)S(1)}, u32[]{:S(2)}, u32[]{:S(2)}) %all-to-all-start.3) | async-done | bytes 196640 | tf_op jit(solution)/shard_map/all_to_all | solution.py:49
  97.7 1.8 reduce.8
  100.3 6.5 %all-to-all-start.4 = ((bf16[32,2,1536]{2,1,0:T(2,128)(2,1)}), bf16[32,2,1536]{2,1,0:T(2,128)(2,1)S(1)}, u32[]{:S(2)}, u32[]{:S(2)}) async-start(bf16[32,2,1536]{2,1,0:T(2,128)(2,1)} %reshape.111), calls=%async_computation.4 | async-start | bytes 393216 | tf_op jit(solution)/shard_map/all_to_all | solution.py:75
  106.8 21.7 %all-gather = bf16[16,32,6]{1,2,0:T(8,128)(2,1)S(1)} all-gather(bf16[1,32,6]{1,2,0:T(8,128)(2,1)S(1)} %get-tuple-element.11), channel_id=1, replica_groups=mesh['row'=16,'col'=32] {'row'}, dimensions={0}, use_global_device_ids=true | all-gather | bytes 6528 | tf_op jit(solution)/shard_map/all_gather | solution.py:25
  129.7 5.0 %fusion = (f32[6,8,32]{2,1,0:T(8,128)S(1)}, f32[6,8,32,512]{3,2,1,0:T(8,128)S(1)}) fusion(f32[6,512]{1,0:T(8,128)S(1)} %bitcast.50, bf16[512,6,8,64]{3,0,2,1:T(8,128)(2,1)} %all-gather.5.cloned.1.call-done, bf16[32,6,8,64]{3,2,0,1:T(8,128)(2,1)S(1)} %reshape.92), kind=kOutput, calls=%fused_computation.2 | convolution fusion | flops 103021056 | bytes 6506496 | tf_op jit(solution)/shard_map/rchd,kchd->chrk/dot_general | solution.py:27
  134.7 0.9 fusion.1
  135.7 4.1 %fusion.16 = bf16[32,6,8,64]{3,0,2,1:T(8,128)(2,1)S(1)} fusion(bf16[512,6,8,64]{3,0,2,1:T(8,128)(2,1)} %all-gather.7.cloned.1.call-done, f32[6,8,32,512]{3,2,1,0:T(8,128)S(1)} %get-tuple-element.16, f32[6,8,32]{2,1,0:T(8,128)S(1)} %broadcast_maximum_fusion, f32[6,512]{1,0:T(8,128)S(1)} %bitcast.52, f32[32,6,8]{0,2,1:T(8,128)S(1)} %bitcast.53), kind=kOutput, calls=%fused_computation.17 | convolution fusion | flops 104005632 | bytes 6512640 | tf_op jit(solution)/shard_map/chrk,kchd->chrd/dot_general | solution.py:34
  140.2 27.8 %all-gather.9.cloned.1.call-done = bf16[1024,1024]{0,1:T(8,128)(2,1)} async-done(((bf16[1024,64]{0,1:T(8,128)(2,1)}), bf16[1024,1024]{0,1:T(8,128)(2,1)}) %all-gather.9.cloned.1.call-update) | async-done | bytes 2097168 | tf_op jit(solution)/shard_map/all_gather | solution.py:80
  168.1 2.4 %convolution_convert_fusion = bf16[192,1024]{1,0:T(8,128)(2,1)S(1)} fusion(bf16[1024,1024]{0,1:T(8,128)(2,1)} %all-gather.9.cloned.1.call-done, bf16[192,512]{1,0:T(8,128)(2,1)S(1)} %bitcast.49, bf16[192,512]{1,0:T(8,128)(2,1)S(1)} %concatenate.8), kind=kOutput, calls=%fused_computation.14 | convolution fusion | flops 403636224 | bytes 2883584 | tf_op jit(solution)/shard_map/dot_general | solution.py:79
  170.6 1.0 copy.70
  (40 shorter events, 7.5 us)
Async XLA Ops:
  6.5 4.4 %copy-start.2 = (s32[32,6]{0,1:T(8,128)S(1)}, s32[32,6]{0,1:T(8,128)}, u32[]{:S(2)}) copy-start(s32[32,6]{0,1:T(8,128)} %param.8) | copy-start | bytes 2308
  6.5 22.4 %copy-start = (bf16[32,6,1024]{2,0,1:T(8,128)(2,1)S(1)}, bf16[32,6,1024]{2,0,1:T(8,128)(2,1)}, u32[]{:S(2)}) copy-start(bf16[32,6,1024]{2,0,1:T(8,128)(2,1)} %param.5) | copy-start | bytes 1179652
  6.5 123.2 %all-gather.5.cloned.1.call-start = ((), (), s32[]{:S(2)}) async-start(), calls=%async_computation.5 | async-start | bytes 6684672 | tf_op jit(solution)/shard_map/all_gather | solution.py:23
  8.7 126.9 %all-gather.7.cloned.1.call-start = ((), (), s32[]{:S(2)}) async-start(), calls=%async_computation.6 | async-start | bytes 6684672 | tf_op jit(solution)/shard_map/all_gather | solution.py:24
  11.6 27.5 %all-to-all-start.2 = ((bf16[32,1,6]{2,1,0:T(2,128)(2,1)}), bf16[32,1,6]{2,1,0:T(2,128)(2,1)S(1)}, u32[]{:S(2)}, u32[]{:S(2)}) async-start(bf16[32,1,6]{2,1,0:T(2,128)(2,1)} %copy.65), calls=%async_computation.2 | async-start | bytes 32768 | tf_op jit(solution)/shard_map/all_to_all | solution.py:52
  28.2 139.9 %all-gather.9.cloned.1.call-start = ((), (), s32[]{:S(2)}) async-start(), calls=%async_computation.7 | async-start | bytes 2228224 | tf_op jit(solution)/shard_map/all_gather | solution.py:80
  39.2 19.5 %all-to-all-start = ((bf16[32,6,512]{2,1,0:T(8,128)(2,1)}), bf16[32,6,512]{2,1,0:T(8,128)(2,1)S(1)}, u32[]{:S(2)}, u32[]{:S(2)}) async-start(bf16[32,6,512]{2,1,0:T(8,128)(2,1)} %copy.74), calls=%async_computation | async-start | bytes 524288 | tf_op jit(solution)/shard_map/all_to_all | solution.py:43
  58.7 19.6 %all-to-all-start.1 = ((bf16[32,6,512]{2,1,0:T(8,128)(2,1)}), bf16[32,6,512]{2,1,0:T(8,128)(2,1)S(1)}, u32[]{:S(2)}, u32[]{:S(2)}) async-start(bf16[32,6,512]{2,1,0:T(8,128)(2,1)} %copy.75), calls=%async_computation.1 | async-start | bytes 524288 | tf_op jit(solution)/shard_map/all_to_all | solution.py:46
  78.3 17.1 %all-to-all-start.3 = ((bf16[32,6,512]{2,1,0:T(8,128)(2,1)}), bf16[32,6,512]{2,1,0:T(8,128)(2,1)S(1)}, u32[]{:S(2)}, u32[]{:S(2)}) async-start(bf16[32,6,512]{2,1,0:T(8,128)(2,1)} %copy.73), calls=%async_computation.3 | async-start | bytes 524288 | tf_op jit(solution)/shard_map/all_to_all | solution.py:49
  100.3 28.6 %all-to-all-start.4 = ((bf16[32,2,1536]{2,1,0:T(2,128)(2,1)}), bf16[32,2,1536]{2,1,0:T(2,128)(2,1)S(1)}, u32[]{:S(2)}, u32[]{:S(2)}) async-start(bf16[32,2,1536]{2,1,0:T(2,128)(2,1)} %reshape.111), calls=%async_computation.4 | async-start | bytes 393216 | tf_op jit(solution)/shard_map/all_to_all | solution.py:75
  135.6 32.4 %copy-start.1 = (bf16[1,192,512]{2,1,0:T(8,128)(2,1)S(1)}, bf16[1,192,512]{2,1,0:T(8,128)(2,1)}, u32[]{:S(2)}) copy-start(bf16[1,192,512]{2,1,0:T(8,128)(2,1)} %copy.92) | copy-start | bytes 589828
Sparse Core Ops, SparseCore 0:
  9.5 61.3 all-gather.4
  72.9 53.8 all-gather.6
  129.0 39.0 all-gather.8
where the time goes:
time: 179 us; the launch traced here: 178 us
  waiting for transfers between devices  78.1 us (44%)
  starting transfers between devices  36.8 us (21%)
  blocking collectives  21.7 us (12%)
  between operations  13.3 us (7%)
  local copies, waits for them, and re-layouts  12.8 us (7%)
  matrix products  12.4 us (7%)
  other arithmetic  2.99 us (2%)
    all_gather x1, waiting for transfers between devices, on_device(): lax.all_gather(w_out, 'row', axis=1, tiled=True)  27.8 us
    all_gather x1, blocking collectives, on_device(): bias_piece = lax.all_gather(key_bias, 'row', axis=0, tiled=True)  21.7 us
    all_to_all x1, starting transfers between devices, on_device(): lax.all_to_all(key_bias, 'col', split_axis=0, concat_axis=1, tiled=True)  16.5 us
    all_to_all x1, waiting for transfers between devices, on_device(): lax.all_to_all(query_tokens[:, :, half_width:], 'col', split_axis=0, conc...  14.8 us
    all_to_all x1, waiting for transfers between devices, on_device(): lax.all_to_all(key_tokens[:, :, half_width:], 'col', split_axis=0, concat...  14.1 us
    all_to_all x1, waiting for transfers between devices, on_device(): lax.all_to_all(value_tokens[:, :, half_width:], 'col', split_axis=0, conc...  11.2 us
    all_to_all x1, waiting for transfers between devices, on_device(): lax.all_to_all(key_bias, 'col', split_axis=0, concat_axis=1, tiled=True)  9.38 us
    all_to_all x1, starting transfers between devices, on_device(): lax.all_to_all(local_rows, 'col', split_axis=1, concat_axis=0, tiled=True)  6.53 us
  transfers between devices with their start and end apart: 8, of which 5 were waited for; matrix products, arithmetic and copies ran while one was open for 13% of the time, Pallas kernels for 0%

commit v1 on v0

v1 whole, which is shorter than its diff:
```python
import jax
import jax.numpy as jnp
from jax import lax
from jax.experimental import pallas as pl
from jax.experimental.pallas import tpu as pltpu
from jax.sharding import PartitionSpec as P

HEADS = 16
HEAD = 64
HALF = HEADS // 2
WIDTH = HALF * HEAD
LOG2E = 1.4426950408889634
VMEM_LIMIT = 48 * 1024 * 1024


def swap_halves(tile):
    return pltpu.roll(tile, HEAD, tile.ndim - 1)


def low_lanes(shape):
    return lax.broadcasted_iota(jnp.int32, shape, len(shape) - 1) < HEAD


def bias_lanes(merges, first_token, first_lane, count):
    tokens, rows = merges.shape
    bias = jnp.log(merges.astype(jnp.float32)).astype(jnp.bfloat16).astype(jnp.float32)
    token = lax.broadcasted_iota(jnp.int32, (tokens, 128), 0) - first_token
    lane = lax.broadcasted_iota(jnp.int32, (tokens, 128), 1) - first_lane
    pick = ((token == lane) & (lane >= 0) & (lane < count)).astype(jnp.float32)
    return lax.dot_general(
        bias.astype(jnp.bfloat16),
        pick.astype(jnp.bfloat16),
        (((0,), (0,)), ((), ())),
        preferred_element_type=jnp.float32,
    )


def pack_rows_kernel(q_ref, k_ref, v_ref, m_ref, out_ref):
    bias = bias_lanes(m_ref[...], 0, 0, 6)
    low = low_lanes((6, 32, 128))
    for pair in range(HALF // 2):
        lanes = slice(128 * pair, 128 * pair + 128)
        q = q_ref[:, :, lanes].astype(jnp.float32)
        k = k_ref[:, :, lanes].astype(jnp.float32)
        v = v_ref[:, :, lanes].astype(jnp.float32)
        sq, sk, sv = swap_halves(q), swap_halves(k), swap_halves(v)
        for odd in range(2):
            qk = jnp.where(low, sq, k) if odd else jnp.where(low, q, sk)
            vv = (
                jnp.where(low[:3], sv[:3], v[3:])
                if odd
                else jnp.where(low[:3], v[:3], sv[3:])
            )
            for rg in range(4):
                rows = slice(8 * rg, 8 * rg + 8)
                block = rg * 8 + 2 * pair + odd
                out_ref[block, 0:6] = qk[:, rows].astype(jnp.bfloat16)
                out_ref[block, 6:9] = vv[:, rows].astype(jnp.bfloat16)
                out_ref[block, 9] = bias[rows].astype(jnp.bfloat16)


def pack_columns_kernel(q_ref, k_ref, v_ref, m_ref, out_ref):
    low = low_lanes((6, 32, 128))
    biases = [bias_lanes(m_ref[...], 3 * g, HEAD, 3) for g in range(2)]
    for pair in range(HALF // 2):
        lanes = slice(128 * pair, 128 * pair + 128)
        q = q_ref[:, :, lanes].astype(jnp.float32)
        k = k_ref[:, :, lanes].astype(jnp.float32)
        v = v_ref[:, :, lanes].astype(jnp.float32)
        sq, sk, sv = swap_halves(q), swap_halves(k), swap_halves(v)
        for odd in range(2):
            qk = jnp.where(low, sq, k) if odd else jnp.where(low, q, sk)
            to_low, to_high = (sv, v) if odd else (v, sv)
            for g in range(2):
                block = 2 * (2 * pair + odd) + g
                out_ref[block, 0:3] = qk[3 * g : 3 * g + 3].astype(jnp.bfloat16)
                out_ref[block, 3] = jnp.where(
                    low[0], to_low[3 * g], to_high[3 * g + 1]
                ).astype(jnp.bfloat16)
                out_ref[block, 4] = jnp.where(
                    low[0], to_low[3 * g + 2], biases[g]
                ).astype(jnp.bfloat16)


def attend(q, k, v, bias):
    scores = lax.dot_general(
        k, q, (((1,), (1,)), ((), ())), preferred_element_type=jnp.float32
    )
    scores = scores * (HEAD**-0.5 * LOG2E) + bias * LOG2E
    weights = jnp.exp2(scores - jnp.max(scores, axis=0, keepdims=True))
    totals = jnp.sum(weights, axis=0, keepdims=True)
    summed = lax.dot_general(
        v,
        weights.astype(jnp.bfloat16),
        (((0,), (0,)), ((), ())),
        preferred_element_type=jnp.float32,
    )
    return summed / totals


def attend_rows_kernel(in_ref, out_ref, qk_ref, v_ref, b_ref, o_ref):
    for t in range(6):
        qk_ref[t * 256 : t * 256 + 256] = (
            in_ref[:, t].astype(jnp.float32).reshape(256, 128)
        )
    for j in range(3):
        v_ref[j * 256 : j * 256 + 256] = (
            in_ref[:, 6 + j].astype(jnp.float32).reshape(256, 128)
        )
    b_ref[...] = in_ref[:, 9].astype(jnp.float32).reshape(256, 128)
    for r in range(8):
        qk = qk_ref[pl.ds(r, 192, stride=8), :].astype(jnp.bfloat16)
        vv = v_ref[pl.ds(r, 96, stride=8), :].astype(jnp.bfloat16)
        bb = b_ref[pl.ds(r, 32, stride=8), :]
        v = jnp.concatenate([vv[:, :HEAD], vv[:, HEAD:]], axis=0)
        bias = jnp.concatenate([bb[:, t : t + 1] for t in range(6)], axis=0)
        out = attend(qk[:, :HEAD], qk[:, HEAD:], v, bias)
        out = out.T
        o_ref[pl.ds(r, 96, stride=8), :] = jnp.concatenate([out[:96], out[96:]], axis=1)
    for j in range(3):
        out_ref[:, j] = (
            o_ref[j * 256 : j * 256 + 256].reshape(32, 8, 128).astype(jnp.bfloat16)
        )


def attend_columns_kernel(in_ref, out_ref):
    tail = in_ref[:, 4].reshape(512, 128)
    vv = in_ref[:, 3].reshape(512, 128)
    values = (vv[:, :HEAD], vv[:, HEAD:], tail[:, :HEAD])
    outs = []
    for j in range(3):
        qk = in_ref[:, j].reshape(512, 128)
        bias = tail[:, HEAD + j : HEAD + j + 1].astype(jnp.float32)
        pieces = [
            attend(qk[start : start + 256, :HEAD], qk[:, HEAD:], values[j], bias)
            for start in (0, 256)
        ]
        outs.append(jnp.concatenate(pieces, axis=1).T)
    out_ref[:, 0:32] = (
        jnp.concatenate([outs[0], outs[1]], axis=1).astype(jnp.bfloat16).reshape(16, 32, 128)
    )
    last = outs[2].reshape(16, 2, 16, HEAD)
    out_ref[:, 32:48] = jnp.concatenate([last[:, 0], last[:, 1]], axis=2).astype(jnp.bfloat16)


def project_kernel(column_ref, row_ref, w_ref, out_ref, joined_ref):
    for pair in range(HALF // 2):
        lanes = slice(128 * pair, 128 * pair + 128)
        for g in range(2):
            even, odd = column_ref[4 * pair + g], column_ref[4 * pair + 2 + g]
            even_last = jnp.concatenate([even[32:, :HEAD], even[32:, HEAD:]], axis=0)
            odd_last = jnp.concatenate([odd[32:, :HEAD], odd[32:, HEAD:]], axis=0)
            joined_ref[3 * g, :, lanes] = jnp.concatenate(
                [even[:32, :HEAD], odd[:32, :HEAD]], axis=1
            )
            joined_ref[3 * g + 1, :, lanes] = jnp.concatenate(
                [even[:32, HEAD:], odd[:32, HEAD:]], axis=1
            )
            joined_ref[3 * g + 2, :, lanes] = jnp.concatenate([even_last, odd_last], axis=1)
        lanes = slice(WIDTH + 128 * pair, WIDTH + 128 * pair + 128)
        for half in range(2):
            blocks = (2 * half, 2 * half + 1)
            even = [row_ref[rg * 8 + 2 * pair].astype(jnp.float32) for rg in blocks]
            odd = [row_ref[rg * 8 + 2 * pair + 1].astype(jnp.float32) for rg in blocks]
            even = jnp.concatenate(even, axis=1)
            odd = jnp.concatenate(odd, axis=1)
            low = low_lanes(even.shape)
            rows = slice(16 * half, 16 * half + 16)
            joined_ref[0:3, rows, lanes] = jnp.where(low, even, swap_halves(odd)).astype(jnp.bfloat16)
            joined_ref[3:6, rows, lanes] = jnp.where(low, swap_halves(even), odd).astype(jnp.bfloat16)
    joined = joined_ref[...].reshape(192, 2 * WIDTH)
    out_ref[...] = (
        lax.dot_general(
            joined, w_ref[...], (((1,), (1,)), ((), ())), preferred_element_type=jnp.float32
        )
        .astype(jnp.bfloat16)
        .reshape(6, 32, 2 * WIDTH)
    )


def kernel_call(kernel, out_shape, name, in_specs, scratch=()):
    vmem = pl.BlockSpec(memory_space=pltpu.VMEM)
    return pl.pallas_call(
        kernel,
        out_shape=jax.ShapeDtypeStruct(out_shape, jnp.bfloat16),
        in_specs=in_specs,
        out_specs=vmem,
        scratch_shapes=list(scratch),
        compiler_params=pltpu.CompilerParams(vmem_limit_bytes=VMEM_LIMIT),
        name=name,
    )


def on_device(query_tokens, key_tokens, value_tokens, merge_sizes, w_out):
    vmem = pl.BlockSpec(memory_space=pltpu.VMEM)
    tokens = [jnp.swapaxes(x, 0, 1) for x in (query_tokens, key_tokens, value_tokens)]
    merges = jnp.transpose(merge_sizes)

    def packed(kernel, which, shape, name):
        return pl.pallas_call(
            kernel,
            out_shape=jax.ShapeDtypeStruct(shape, jnp.bfloat16),
            grid=(1,),
            in_specs=[pl.BlockSpec((6, 32, WIDTH), lambda i: (0, 0, which))] * 3
            + [pl.BlockSpec((6, 32), lambda i: (0, 0))],
            out_specs=pl.BlockSpec(shape, lambda i: (0,) * len(shape)),
            compiler_params=pltpu.CompilerParams(vmem_limit_bytes=VMEM_LIMIT),
            name=name,
        )(*tokens, merges)

    weights = lax.all_gather(jnp.transpose(w_out), "row", axis=0, tiled=True)
    row_packed = packed(pack_rows_kernel, 1, (32, 10, 8, 128), "pack_rows")
    row_moved = lax.all_to_all(row_packed, "col", 0, 0, tiled=True)
    column_packed = packed(pack_columns_kernel, 0, (16, 5, 32, 128), "pack_columns")
    column_moved = lax.all_to_all(column_packed, "row", 0, 0, tiled=True)
    row_out = kernel_call(
        attend_rows_kernel,
        (32, 3, 8, 128),
        "attend_rows",
        [vmem],
        [
            pltpu.VMEM((1536, 128), jnp.float32),
            pltpu.VMEM((768, 128), jnp.float32),
            pltpu.VMEM((256, 128), jnp.float32),
            pltpu.VMEM((768, 128), jnp.float32),
        ],
    )(row_moved)
    row_back = lax.all_to_all(row_out, "col", 0, 0, tiled=True)
    column_out = kernel_call(attend_columns_kernel, (16, 48, 128), "attend_columns", [vmem])(
        column_moved
    )
    column_back = lax.all_to_all(column_out, "row", 0, 0, tiled=True)
    mixed = kernel_call(
        project_kernel,
        (6, 32, 2 * WIDTH),
        "project",
        [vmem] * 3,
        [pltpu.VMEM((6, 32, 2 * WIDTH), jnp.bfloat16)],
    )(column_back, row_back, weights)
    return jnp.swapaxes(mixed, 0, 1)


def solution(mesh):
    return jax.shard_map(
        on_device,
        mesh=mesh,
        in_specs=(
            P("row", "col", None),
            P("row", "col", None),
            P("row", "col", None),
            P("row", "col"),
            P(None, "row"),
        ),
        out_specs=P("row", "col", None),
        check_vma=False,
    )
```

time: 179 us -> 110 us (0.61)
  the two profiles are of different devices: /device:TPU:1 before, /device:TPU:8 now
where the time goes in v1:
time: 110 us; the launch traced here: 109 us
  waiting for transfers between devices  34.8 us (32%)
  starting transfers between devices  27 us (25%)
  blocking collectives  19.1 us (17%)
  between operations  13.5 us (12%)
  Pallas kernels  9.47 us (9%)
  local copies, waits for them, and re-layouts  5.27 us (5%)
    all_to_all x1, waiting for transfers between devices, on_device(): row_moved = lax.all_to_all(row_packed, 'col', 0, 0, tiled=True)  19.5 us
    all_to_all x1, blocking collectives, on_device(): row_back = lax.all_to_all(row_out, 'col', 0, 0, tiled=True)  19.1 us
    all_to_all x1, starting transfers between devices, on_device(): row_moved = lax.all_to_all(row_packed, 'col', 0, 0, tiled=True)  12.2 us
    all_to_all x1, waiting for transfers between devices, on_device(): column_moved = lax.all_to_all(column_packed, 'row', 0, 0, tiled=True)  10.6 us
    all_to_all x1, starting transfers between devices, on_device(): column_moved = lax.all_to_all(column_packed, 'row', 0, 0, tiled=True)  9.25 us
    all_to_all x1, starting transfers between devices, on_device(): column_back = lax.all_to_all(column_out, 'row', 0, 0, tiled=True)  5.61 us
    unnamed x18, local copies, waits for them, and re-layouts  5.27 us
    all_to_all x1, waiting for transfers between devices, on_device(): column_back = lax.all_to_all(column_out, 'row', 0, 0, tiled=True)  4 us
  transfers between devices with their start and end apart: 4, of which 3 were waited for; matrix products, arithmetic and copies ran while one was open for 0% of the time, Pallas kernels for 7%

profile of v1, /device:TPU:8, one launch (start us, length us, event | category | flops | bytes accessed | tf_op | source)
XLA Modules:
  0.0 109.1 jit_solution(4278238211000798209)
XLA Ops:
  6.5 0.0 all-gather.2.cloned.1.call-start
  6.5 0.7 all-gather.2.cloned.1.call-update
  7.3 0.0 copy-start.1
  7.3 1.0 copy-done.1
  8.3 1.0 copy-done.3
  9.3 1.0 copy-done.5
  10.2 0.7 copy-done.7
  10.9 1.1 %pack_columns.1 = bf16[16,5,32,128]{3,2,1,0:T(8,128)(2,1)} custom-call(bf16[6,32,1024]{2,1,0:T(8,128)(2,1)S(1)} %bitcast.6, bf16[6,32,1024]{2,1,0:T(8,128)(2,1)S(1)} %bitcast.8, bf16[6,32,1024]{2,1,0:T(8,128)(2,1)S(1)} %bitcast.10, s32[6,32]{1,0:T(8,128)S(1)} %bitcast.12), custom_call_target="tpu_custom_call" | custom-call | tf_op jit(solution)/shard_map/pack_columns/pallas_call | solution.py:200
  12.1 9.3 %all-to-all-start = ((bf16[16,5,32,128]{3,2,1,0:T(8,128)(2,1)}), bf16[16,5,32,128]{3,2,1,0:T(8,128)(2,1)S(1)}, u32[]{:S(2)}, u32[]{:S(2)}) async-start(bf16[16,5,32,128]{3,2,1,0:T(8,128)(2,1)} %pack_columns.1), calls=%async_computation | async-start | bytes 1310720 | tf_op jit(solution)/shard_map/all_to_all | solution.py:215
  21.3 0.0 copy-done.8
  21.3 0.0 copy-done.2
  21.3 0.0 copy-done.4
  21.3 0.0 copy-done.6
  21.3 1.1 %pack_rows.1 = bf16[32,10,8,128]{3,2,1,0:T(8,128)(2,1)} custom-call(bf16[6,32,1024]{2,1,0:T(8,128)(2,1)S(1)} %bitcast.7, bf16[6,32,1024]{2,1,0:T(8,128)(2,1)S(1)} %bitcast.9, bf16[6,32,1024]{2,1,0:T(8,128)(2,1)S(1)} %bitcast.11, s32[6,32]{1,0:T(8,128)S(1)} %bitcast.13), custom_call_target="tpu_custom_call" | custom-call | tf_op jit(solution)/shard_map/pack_rows/pallas_call | solution.py:200
  22.5 10.6 %all-to-all-done.in_ref = bf16[16,5,32,128]{3,2,1,0:T(8,128)(2,1)S(1)} async-done(((bf16[16,5,32,128]{3,2,1,0:T(8,128)(2,1)}), bf16[16,5,32,128]{3,2,1,0:T(8,128)(2,1)S(1)}, u32[]{:S(2)}, u32[]{:S(2)}) %all-to-all-start) | async-done | bytes 655392 | tf_op jit(solution)/shard_map/all_to_all | solution.py:215
  33.0 12.2 %all-to-all-start.2 = ((bf16[32,10,8,128]{3,2,1,0:T(8,128)(2,1)}), bf16[32,10,8,128]{3,2,1,0:T(8,128)(2,1)S(1)}, u32[]{:S(2)}, u32[]{:S(2)}) async-start(bf16[32,10,8,128]{3,2,1,0:T(8,128)(2,1)} %pack_rows.1), calls=%async_computation.2 | async-start | bytes 1310720 | tf_op jit(solution)/shard_map/all_to_all | solution.py:213
  45.2 3.5 %attend_columns.1 = bf16[16,48,128]{2,1,0:T(8,128)(2,1)} custom-call(bf16[16,5,32,128]{3,2,1,0:T(8,128)(2,1)S(1)} %all-to-all-done.in_ref), custom_call_target="tpu_custom_call" | custom-call | tf_op jit(solution)/shard_map/attend_columns/pallas_call | solution.py:229
  48.7 19.5 %all-to-all-done.2.in_ref = bf16[32,10,8,128]{3,2,1,0:T(8,128)(2,1)S(1)} async-done(((bf16[32,10,8,128]{3,2,1,0:T(8,128)(2,1)}), bf16[32,10,8,128]{3,2,1,0:T(8,128)(2,1)S(1)}, u32[]{:S(2)}, u32[]{:S(2)}) %all-to-all-start.2) | async-done | bytes 655392 | tf_op jit(solution)/shard_map/all_to_all | solution.py:213
  68.2 5.6 %all-to-all-start.1 = ((bf16[16,48,128]{2,1,0:T(8,128)(2,1)}), bf16[16,48,128]{2,1,0:T(8,128)(2,1)S(1)}, u32[]{:S(2)}, u32[]{:S(2)}) async-start(bf16[16,48,128]{2,1,0:T(8,128)(2,1)} %attend_columns.1), calls=%async_computation.1 | async-start | bytes 393216 | tf_op jit(solution)/shard_map/all_to_all | solution.py:232
  73.8 2.1 %attend_rows.1 = bf16[32,3,8,128]{3,2,1,0:T(8,128)(2,1)S(1)} custom-call(bf16[32,10,8,128]{3,2,1,0:T(8,128)(2,1)S(1)} %all-to-all-done.2.in_ref), custom_call_target="tpu_custom_call" | custom-call | tf_op jit(solution)/shard_map/attend_rows/pallas_call | solution.py:216
  75.9 4.0 %all-to-all-done.1.column_ref = bf16[16,48,128]{2,1,0:T(8,128)(2,1)S(1)} async-done(((bf16[16,48,128]{2,1,0:T(8,128)(2,1)}), bf16[16,48,128]{2,1,0:T(8,128)(2,1)S(1)}, u32[]{:S(2)}, u32[]{:S(2)}) %all-to-all-start.1) | async-done | bytes 196640 | tf_op jit(solution)/shard_map/all_to_all | solution.py:232
  79.9 19.1 %all_to_all.20.row_ref = bf16[32,3,8,128]{3,2,1,0:T(8,128)(2,1)S(1)} all-to-all(bf16[32,3,8,128]{3,2,1,0:T(8,128)(2,1)S(1)} %attend_rows.1), channel_id=1, replica_groups=mesh['row'=16,'col'=32] {'col'}, dimensions={0} | all-to-all | bytes 393216 | tf_op jit(solution)/shard_map/all_to_all | solution.py:228
  99.0 1.6 %copy-done = bf16[1024,1024]{1,0:T(8,128)(2,1)S(1)} copy-done((bf16[1024,1024]{1,0:T(8,128)(2,1)S(1)}, bf16[1024,1024]{1,0:T(8,128)(2,1)}, u32[]{:S(2)}) %copy-start) | copy-done | bytes 2097176
  100.6 1.7 %project.1 = bf16[6,32,1024]{2,1,0:T(8,128)(2,1)} custom-call(bf16[16,48,128]{2,1,0:T(8,128)(2,1)S(1)} %all-to-all-done.1.column_ref, bf16[32,3,8,128]{3,2,1,0:T(8,128)(2,1)S(1)} %all_to_all.20.row_ref, bf16[1024,1024]{1,0:T(8,128)(2,1)S(1)} %copy-done), custom_call_target="tpu_custom_call" | custom-call | tf_op jit(solution)/shard_map/project/pallas_call | solution.py:233
  (9 shorter events, 0.0 us)
Async XLA Ops:
  6.5 14.8 %copy-start.8 = (s32[32,6]{0,1:T(8,128)S(1)}, s32[32,6]{0,1:T(8,128)}, u32[]{:S(2)}) copy-start(s32[32,6]{0,1:T(8,128)} %param.8) | copy-start | bytes 2308
  6.5 92.4 %all-gather.2.cloned.1.call-start = ((), (), s32[]{:S(2)}) async-start(), calls=%async_computation.4 | async-start | bytes 2228224 | tf_op jit(solution)/shard_map/all_gather | solution.py:211
  7.3 1.0 copy-start.1
  8.3 1.0 copy-start.3
  9.3 1.0 copy-start.5
  10.2 0.7 copy-start.7
  10.9 10.4 %copy-start.2 = (bf16[32,6,1024]{2,0,1:T(8,128)(2,1)S(1)}, bf16[32,6,1024]{2,0,1:T(8,128)(2,1)}, u32[]{:S(2)}) copy-start(bf16[32,6,1024]{2,0,1:T(8,128)(2,1)} %param.5) | copy-start | bytes 1179652
  10.9 10.4 %copy-start.4 = (bf16[32,6,1024]{2,0,1:T(8,128)(2,1)S(1)}, bf16[32,6,1024]{2,0,1:T(8,128)(2,1)}, u32[]{:S(2)}) copy-start(bf16[32,6,1024]{2,0,1:T(8,128)(2,1)} %param.6) | copy-start | bytes 1179652
  10.9 10.4 %copy-start.6 = (bf16[32,6,1024]{2,0,1:T(8,128)(2,1)S(1)}, bf16[32,6,1024]{2,0,1:T(8,128)(2,1)}, u32[]{:S(2)}) copy-start(bf16[32,6,1024]{2,0,1:T(8,128)(2,1)} %param.7) | copy-start | bytes 1179652
  12.1 21.0 %all-to-all-start = ((bf16[16,5,32,128]{3,2,1,0:T(8,128)(2,1)}), bf16[16,5,32,128]{3,2,1,0:T(8,128)(2,1)S(1)}, u32[]{:S(2)}, u32[]{:S(2)}) async-start(bf16[16,5,32,128]{3,2,1,0:T(8,128)(2,1)} %pack_columns.1), calls=%async_computation | async-start | bytes 1310720 | tf_op jit(solution)/shard_map/all_to_all | solution.py:215
  33.0 35.2 %all-to-all-start.2 = ((bf16[32,10,8,128]{3,2,1,0:T(8,128)(2,1)}), bf16[32,10,8,128]{3,2,1,0:T(8,128)(2,1)S(1)}, u32[]{:S(2)}, u32[]{:S(2)}) async-start(bf16[32,10,8,128]{3,2,1,0:T(8,128)(2,1)} %pack_rows.1), calls=%async_computation.2 | async-start | bytes 1310720 | tf_op jit(solution)/shard_map/all_to_all | solution.py:213
  68.2 11.7 %all-to-all-start.1 = ((bf16[16,48,128]{2,1,0:T(8,128)(2,1)}), bf16[16,48,128]{2,1,0:T(8,128)(2,1)S(1)}, u32[]{:S(2)}, u32[]{:S(2)}) async-start(bf16[16,48,128]{2,1,0:T(8,128)(2,1)} %attend_columns.1), calls=%async_computation.1 | async-start | bytes 393216 | tf_op jit(solution)/shard_map/all_to_all | solution.py:232
  99.0 1.6 %copy-start = (bf16[1024,1024]{1,0:T(8,128)(2,1)S(1)}, bf16[1024,1024]{1,0:T(8,128)(2,1)}, u32[]{:S(2)}) copy-start(bf16[1024,1024]{1,0:T(8,128)(2,1)} %all-gather.2.cloned.1.call-done.w_ref) | copy-start | bytes 6291460
Sparse Core Ops, SparseCore 0:
  9.5 48.4 all-gather.1

commit v2 on v1

v2 whole, which is shorter than its diff:
```python
import jax
import jax.numpy as jnp
from jax import lax
from jax.experimental import pallas as pl
from jax.experimental.pallas import tpu as pltpu
from jax.sharding import PartitionSpec as P

HEADS = 16
HEAD = 64
HALF = HEADS // 2
WIDTH = HALF * HEAD
UNIT = 10
W_TILES = 16
SAME_CORE = [list(range(core, 16, 2)) for core in range(2)]
LOG2E = 1.4426950408889634
VMEM_LIMIT = 16 * 1024 * 1024


def swap_halves(tile):
    return pltpu.roll(tile, HEAD, tile.ndim - 1)


def low_lanes(shape):
    return lax.broadcasted_iota(jnp.int32, shape, len(shape) - 1) < HEAD


def bias_lanes(merges, first_token, first_lane, count):
    tokens, rows = merges.shape
    bias = jnp.log(merges.astype(jnp.float32)).astype(jnp.bfloat16).astype(jnp.float32)
    token = lax.broadcasted_iota(jnp.int32, (tokens, 128), 0) - first_token
    lane = lax.broadcasted_iota(jnp.int32, (tokens, 128), 1) - first_lane
    pick = ((token == lane) & (lane >= 0) & (lane < count)).astype(jnp.float32)
    return lax.dot_general(
        bias.astype(jnp.bfloat16),
        pick.astype(jnp.bfloat16),
        (((0,), (0,)), ((), ())),
        preferred_element_type=jnp.float32,
    )


def fetch(sources, targets, sems):
    copies = [
        pltpu.make_async_copy(source, target, sems.at[n])
        for n, (source, target) in enumerate(zip(sources, targets))
    ]
    for copy in copies:
        copy.start()
    for copy in copies:
        copy.wait()


def pack_rows_kernel(q_ref, k_ref, v_ref, m_hbm, out_ref, m_ref, sems):
    fetch([m_hbm], [m_ref], sems)
    bias = bias_lanes(m_ref[...], 0, 0, 6)
    low = low_lanes((6, 32, 128))
    for pair in range(HALF // 2):
        lanes = slice(128 * pair, 128 * pair + 128)
        q = q_ref[:, :, lanes].astype(jnp.float32)
        k = k_ref[:, :, lanes].astype(jnp.float32)
        v = v_ref[:, :, lanes].astype(jnp.float32)
        sq, sk, sv = swap_halves(q), swap_halves(k), swap_halves(v)
        for odd in range(2):
            qk = jnp.where(low, sq, k) if odd else jnp.where(low, q, sk)
            vv = (
                jnp.where(low[:3], sv[:3], v[3:])
                if odd
                else jnp.where(low[:3], v[:3], sv[3:])
            )
            for rg in range(4):
                rows = slice(8 * rg, 8 * rg + 8)
                block = rg * 8 + 2 * pair + odd
                out_ref[block, 0:6] = qk[:, rows].astype(jnp.bfloat16)
                out_ref[block, 6:9] = vv[:, rows].astype(jnp.bfloat16)
                out_ref[block, 9] = bias[rows].astype(jnp.bfloat16)


def place():
    me = lax.axis_index("row")
    return me // 8, (me // 2) % 4, me % 2


def pack_tiles_kernel(q_hbm, k_hbm, v_hbm, m_hbm, w_hbm, send_ref, keep_ref, *refs):
    (*row_refs, m_ref, sems), (y, _, _) = refs, place()
    copies = [(m_hbm, m_ref)]
    for source, target in zip((q_hbm, k_hbm, v_hbm), row_refs):
        copies.append((source.at[:, :, pl.ds(WIDTH, WIDTH)], target))
    for ref, half in ((send_ref, 1 - y), (keep_ref, y)):
        columns = pl.ds(3 * half, 3)
        for pair in range(4):
            for n, source in enumerate((q_hbm, k_hbm, v_hbm)):
                first = UNIT * pair + 3 * n
                lanes = pl.ds(128 * pair, 128)
                copies.append((source.at[columns, :, lanes], ref.at[first : first + 3]))
    for n in range(W_TILES):
        rows, lanes = pl.ds(n % 2 * 32, 32), pl.ds(n // 2 * 128, 128)
        copies.append((w_hbm.at[rows, lanes], send_ref.at[4 * UNIT + n]))
    fetch(*zip(*copies), sems)
    for ref, half in ((send_ref, 1 - y), (keep_ref, y)):
        bias = bias_lanes(m_ref[...], 3 * half, 0, 3).astype(jnp.bfloat16)
        for pair in range(4):
            ref[UNIT * pair + UNIT - 1] = bias


def gather_x_kernel(sent_ref, own_ref, other_ref, *out_refs):
    _, x, _ = place()
    for dx, out_ref in enumerate(out_refs):
        pair = pl.ds((x + dx) % 4 * UNIT, UNIT)
        out_ref[0:UNIT] = own_ref[pair]
        out_ref[UNIT : 2 * UNIT] = other_ref[pair]
        if dx % 2:
            out_ref[2 * UNIT : 2 * UNIT + W_TILES] = sent_ref[4 * UNIT :]
            out_ref[2 * UNIT + W_TILES :] = other_ref[4 * UNIT :]


def early_weights_kernel(sent_ref, other_ref, left_ref, right_ref, early_ref, lack_ref):
    _, x, _ = place()
    early_ref[0:W_TILES] = sent_ref[4 * UNIT :]
    early_ref[W_TILES : 2 * W_TILES] = other_ref[4 * UNIT :]
    early_ref[2 * W_TILES : 4 * W_TILES] = left_ref[2 * UNIT :]
    early_ref[4 * W_TILES :] = right_ref[2 * UNIT :]
    lack_ref[...] = early_ref[pl.ds((2 + 2 * (x % 2)) * W_TILES, 2 * W_TILES)]


def stack_keys_kernel(*refs):
    for dx in range(4):
        for s in range(2):
            first = 14 * dx + 7 * s
            refs[4][first : first + 7] = refs[dx][UNIT * s + 3 : UNIT * s + UNIT]


def assemble_weights_kernel(early_ref, early_other_ref, late_ref, late_other_ref, w_ref):
    y, x, core = place()
    for dc, early, late in ((0, early_ref, late_ref), (1, early_other_ref, late_other_ref)):
        for block in range(8):
            there = (x + (0, 3, 1, 2)[block // 2]) % 4
            part = ((y + block % 2) % 2 * 4 + there) * 2 + (core + dc) % 2
            for n in range(W_TILES):
                rows = pl.ds(pl.multiple_of(part * 64 + n % 2 * 32, 32), 32)
                tile = W_TILES * block + n
                tile = early[tile] if block < 6 else late[tile - 6 * W_TILES]
                w_ref[rows, n // 2 * 128 : n // 2 * 128 + 128] = tile


def attend(q, k, v, bias):
    scores = lax.dot_general(
        k, q, (((1,), (1,)), ((), ())), preferred_element_type=jnp.float32
    )
    scores = scores * (HEAD**-0.5 * LOG2E) + bias * LOG2E
    weights = jnp.exp2(scores - jnp.max(scores, axis=0, keepdims=True))
    totals = jnp.sum(weights, axis=0, keepdims=True)
    summed = lax.dot_general(
        v,
        weights.astype(jnp.bfloat16),
        (((0,), (0,)), ((), ())),
        preferred_element_type=jnp.float32,
    )
    return summed / totals


def attend_rows_kernel(in_ref, after_ref, out_ref, qk_ref, v_ref, b_ref, o_ref):
    for t in range(6):
        qk_ref[t * 256 : t * 256 + 256] = (
            in_ref[:, t].astype(jnp.float32).reshape(256, 128)
        )
    for j in range(3):
        v_ref[j * 256 : j * 256 + 256] = (
            in_ref[:, 6 + j].astype(jnp.float32).reshape(256, 128)
        )
    b_ref[...] = in_ref[:, 9].astype(jnp.float32).reshape(256, 128)
    for r in range(8):
        qk = qk_ref[pl.ds(r, 192, stride=8), :].astype(jnp.bfloat16)
        vv = v_ref[pl.ds(r, 96, stride=8), :].astype(jnp.bfloat16)
        bb = b_ref[pl.ds(r, 32, stride=8), :]
        v = jnp.concatenate([vv[:, :HEAD], vv[:, HEAD:]], axis=0)
        bias = jnp.concatenate([bb[:, t : t + 1] for t in range(6)], axis=0)
        out = attend(qk[:, :HEAD], qk[:, HEAD:], v, bias)
        out = out.T
        o_ref[pl.ds(r, 96, stride=8), :] = jnp.concatenate([out[:96], out[96:]], axis=1)
    for j in range(3):
        out_ref[:, j] = (
            o_ref[j * 256 : j * 256 + 256].reshape(32, 8, 128).astype(jnp.bfloat16)
        )


def attend_columns_kernel(*refs):
    in_refs, other_ref, out_ref = refs[:4], refs[4], refs[5]
    y, x, _ = place()
    sources = [(dx, s) for dx in range(4) for s in range(2)]

    def keys_of(n):
        tiles = [in_refs[dx][UNIT * s + 3 + n] for dx, s in sources]
        tiles += [other_ref[14 * dx + 7 * s + n] for dx, s in sources]
        return jnp.concatenate(tiles, axis=0)

    biases = keys_of(6).astype(jnp.float32) * LOG2E
    low = low_lanes((256, 128))
    for j in range(3):
        q = jnp.concatenate([in_refs[dx][UNIT * s + j] for dx, s in sources], axis=0)
        zero = jnp.zeros_like(q)
        q = jnp.concatenate([jnp.where(low, q, zero), jnp.where(low, zero, q)], axis=0)
        scores = lax.dot_general(
            keys_of(j), q, (((1,), (1,)), ((), ())), preferred_element_type=jnp.float32
        )
        scores = scores * (HEAD**-0.5 * LOG2E) + biases[:, j : j + 1]
        weights = jnp.exp2(scores - jnp.max(scores, axis=0, keepdims=True))
        totals = jnp.sum(weights, axis=0, keepdims=True)
        summed = lax.dot_general(
            keys_of(3 + j),
            weights.astype(jnp.bfloat16),
            (((0,), (0,)), ((), ())),
            preferred_element_type=jnp.float32,
        )
        summed = summed / totals
        out = jnp.concatenate([summed[:HEAD, :256], summed[HEAD:, 256:]], axis=0).T
        out = out.astype(jnp.bfloat16)
        for n, (dx, s) in enumerate(sources):
            out_ref[(y + s) % 2 * 4 + (x - dx + 4) % 4, j] = out[32 * n : 32 * n + 32]


def project_kernel(column_ref, row_ref, w_ref, out_ref, joined_ref):
    for block in range(8):
        lanes = slice(block % 4 * 128, block % 4 * 128 + 128)
        joined_ref[block // 4 * 3 : block // 4 * 3 + 3, :, lanes] = column_ref[block]
    for pair in range(HALF // 2):
        lanes = slice(WIDTH + 128 * pair, WIDTH + 128 * pair + 128)
        for half in range(2):
            blocks = (2 * half, 2 * half + 1)
            even = [row_ref[rg * 8 + 2 * pair].astype(jnp.float32) for rg in blocks]
            odd = [row_ref[rg * 8 + 2 * pair + 1].astype(jnp.float32) for rg in blocks]
            even = jnp.concatenate(even, axis=1)
            odd = jnp.concatenate(odd, axis=1)
            low = low_lanes(even.shape)
            rows = slice(16 * half, 16 * half + 16)
            joined_ref[0:3, rows, lanes] = jnp.where(low, even, swap_halves(odd)).astype(jnp.bfloat16)
            joined_ref[3:6, rows, lanes] = jnp.where(low, swap_halves(even), odd).astype(jnp.bfloat16)
    mixed = lax.dot_general(
        joined_ref[...].reshape(192, 2 * WIDTH),
        w_ref[...],
        (((1,), (1,)), ((), ())),
        preferred_element_type=jnp.float32,
    )
    out_ref[...] = mixed.astype(jnp.bfloat16).reshape(6, 32, 2 * WIDTH)


def call(kernel, out_shapes, name, in_specs, scratch=()):
    vmem = pl.BlockSpec(memory_space=pltpu.VMEM)
    shapes = [jax.ShapeDtypeStruct(shape, jnp.bfloat16) for shape in out_shapes]
    return pl.pallas_call(
        kernel,
        out_shape=shapes,
        in_specs=in_specs,
        out_specs=[vmem] * len(shapes),
        scratch_shapes=list(scratch),
        compiler_params=pltpu.CompilerParams(vmem_limit_bytes=VMEM_LIMIT),
        name=name,
    )


def across_y(array):
    return lax.ppermute(array, "row", [(i, (i + 8) % 16) for i in range(16)])


def across_core(array):
    return lax.ppermute(array, "row", [(i, i // 2 * 2 + (i + 1) % 2) for i in range(16)])


def along_x(array, dx):
    pairs = [(i, i // 8 * 8 + ((i // 2 + dx) % 4) * 2 + i % 2) for i in range(16)]
    return lax.ppermute(array, "row", pairs)


def swap_x(array):
    return lax.ppermute(array, "row", [(i, i ^ 2) for i in range(16)])


def on_device(query_tokens, key_tokens, value_tokens, merge_sizes, w_out):
    vmem = pl.BlockSpec(memory_space=pltpu.VMEM)
    anywhere = pl.BlockSpec(memory_space=pl.ANY)
    hbm = pl.BlockSpec(memory_space=pltpu.HBM)
    tokens = [
        pltpu.with_memory_space_constraint(jnp.swapaxes(x, 0, 1), pltpu.HBM)
        for x in (query_tokens, key_tokens, value_tokens)
    ]
    merges = pltpu.with_memory_space_constraint(jnp.transpose(merge_sizes), pltpu.HBM)
    w_part = pltpu.with_memory_space_constraint(jnp.transpose(w_out), pltpu.HBM)
    sent, own, *row_halves = call(
        pack_tiles_kernel,
        [(4 * UNIT + W_TILES, 32, 128), (4 * UNIT, 32, 128)] + [(6, 32, WIDTH)] * 3,
        "pack_tiles",
        [hbm] * 5,
        [pltpu.VMEM((6, 32), jnp.int32), pltpu.SemaphoreType.DMA((44,))],
    )(*tokens, merges, w_part)
    other = across_y(sent)
    (row_packed,) = call(
        pack_rows_kernel,
        [(32, 10, 8, 128)],
        "pack_rows",
        [vmem] * 3 + [hbm],
        [pltpu.VMEM((6, 32), jnp.int32), pltpu.SemaphoreType.DMA((1,))],
    )(*row_halves, merges)
    row_moved = lax.all_to_all(row_packed, "col", 0, 0, tiled=True)
    by_x = call(
        gather_x_kernel,
        [(2 * UNIT + dx % 2 * 2 * W_TILES, 32, 128) for dx in range(4)],
        "gather_x",
        [vmem] * 3,
    )(sent, own, other)
    by_x = [by_x[0]] + [along_x(by_x[dx], dx) for dx in (1, 2, 3)]
    (keys,) = call(stack_keys_kernel, [(56, 32, 128)], "stack_keys", [vmem] * 4)(*by_x)
    other_keys = across_core(keys)
    early, lack = call(
        early_weights_kernel,
        [(6 * W_TILES, 32, 128), (2 * W_TILES, 32, 128)],
        "early_weights",
        [vmem] * 4,
    )(sent, other, by_x[1], by_x[3])
    late = swap_x(lack)
    weights = [early, across_core(early), late, across_core(late)]
    weights = [pltpu.with_memory_space_constraint(x, pltpu.HBM) for x in weights]
    (column_out,) = call(attend_columns_kernel, [(8, 3, 32, 128)], "attend_columns", [vmem] * 5)(
        *by_x, other_keys
    )
    column_done = column_out
    column_out = lax.all_to_all(
        column_out, "row", 0, 0, tiled=True, axis_index_groups=SAME_CORE
    )
    (row_out,) = call(
        attend_rows_kernel,
        [(32, 3, 8, 128)],
        "attend_rows",
        [vmem, anywhere],
        [
            pltpu.VMEM((1536, 128), jnp.float32),
            pltpu.VMEM((768, 128), jnp.float32),
            pltpu.VMEM((256, 128), jnp.float32),
            pltpu.VMEM((768, 128), jnp.float32),
        ],
    )(row_moved, column_done)
    (weights,) = call(
        assemble_weights_kernel, [(2 * WIDTH, 2 * WIDTH)], "assemble_weights", [vmem] * 4
    )(*weights)
    row_back = lax.all_to_all(row_out, "col", 0, 0, tiled=True)
    (mixed,) = call(
        project_kernel,
        [(6, 32, 2 * WIDTH)],
        "project",
        [vmem] * 3,
        [pltpu.VMEM((6, 32, 2 * WIDTH), jnp.bfloat16)],
    )(column_out, row_back, weights)
    return jnp.swapaxes(mixed, 0, 1)


def solution(mesh):
    return jax.shard_map(
        on_device,
        mesh=mesh,
        in_specs=(
            P("row", "col", None),
            P("row", "col", None),
            P("row", "col", None),
            P("row", "col"),
            P(None, "row"),
        ),
        out_specs=P("row", "col", None),
        check_vma=False,
    )
```

time: 110 us -> 87.2 us (0.79)
  starting transfers between devices: 27 us -> 57 us
  blocking collectives: 19.1 us -> 0 us
  waiting for transfers between devices: 34.8 us -> 16.1 us
  between operations: 13.5 us -> 0.18 us
  local copies, waits for them, and re-layouts: 5.27 us -> 0.7 us
  Pallas kernels: 9.47 us -> 12.5 us
    ppermute x0 -> x8, starting transfers between devices: none -> 28.1 us  [the longest x3 10.8 us: along_x(): return lax.ppermute(array, 'row', pairs)]
    all_to_all x1, waiting for transfers between devices: 19.5 us -> 0.01 us  [on_device(): row_moved = lax.all_to_all(row_packed, 'col', 0, 0, tiled=True)]
    all_to_all x1 -> x0, blocking collectives: 19.1 us -> none  [on_device(): row_back = lax.all_to_all(row_out, 'col', 0, 0, tiled=True)]
    ppermute x0 -> x8, waiting for transfers between devices: none -> 9.53 us  [the longest x3 8.02 us: along_x(): return lax.ppermute(array, 'row', pairs)]
    all_to_all x2, waiting for transfers between devices: 14.6 us -> 6.53 us  [the longest x1 6.53 us: on_device(): row_back = lax.all_to_all(row_out, 'col', 0, 0, tiled=True)]
    unnamed x18 -> x6, local copies, waits for them, and re-layouts: 5.27 us -> 0.7 us
    all_to_all x2, starting transfers between devices: 14.9 us -> 18.3 us  [the longest x1 11.9 us: on_device(): row_back = lax.all_to_all(row_out, 'col', 0, 0, tiled=True)]
    pallas_call x5 -> x9, Pallas kernels: 9.47 us -> 12.5 us  [the longest x1 2.84 us: on_device(): call(attend_rows_kernel, [(32, 3, 8, 128)], 'attend_rows', [vmem, anywher...]
  transfers between devices with their start and end apart: 4 -> 11, of which waited for: 3 -> 4; matrix products, arithmetic and copies ran while one was open for 0% -> 0% of each run, Pallas kernels for 7% -> 10%
where the time goes in v2:
time: 87.2 us; the launch traced here: 86.5 us
  starting transfers between devices  57 us (65%)
  waiting for transfers between devices  16.1 us (18%)
  Pallas kernels  12.5 us (14%)
    all_to_all x1, starting transfers between devices, on_device(): row_back = lax.all_to_all(row_out, 'col', 0, 0, tiled=True)  11.9 us
    ppermute x3, starting transfers between devices, along_x(): return lax.ppermute(array, 'row', pairs)  10.8 us
    all_to_all x1, starting transfers between devices, on_device(): row_moved = lax.all_to_all(row_packed, 'col', 0, 0, tiled=True)  10.6 us
    ppermute x3, waiting for transfers between devices, along_x(): return lax.ppermute(array, 'row', pairs)  8.02 us
    ppermute x1, starting transfers between devices, across_y(): return lax.ppermute(array, 'row', [(i, (i + 8) % 16) for i in range(16)])  7.73 us
    all_to_all x1, waiting for transfers between devices, on_device(): row_back = lax.all_to_all(row_out, 'col', 0, 0, tiled=True)  6.53 us
    all_to_all x1, starting transfers between devices, on_device(): lax.all_to_all(column_out, 'row', 0, 0, tiled=True, axis_index_groups=SAM...  6.4 us
    ppermute x3, starting transfers between devices, across_core(): lax.ppermute(array, 'row', [(i, i // 2 * 2 + (i + 1) % 2) for i in range(...  6.25 us
  transfers between devices with their start and end apart: 11, of which 4 were waited for; matrix products, arithmetic and copies ran while one was open for 0% of the time, Pallas kernels for 10%

profile of v2, /device:TPU:8, one launch (start us, length us, event | category | flops | bytes accessed | tf_op | source)
XLA Modules:
  0.0 86.5 jit_solution(2993928859659597047)
XLA Ops:
  0.0 1.9 %pack_tiles.1 = (bf16[56,32,128]{2,1,0:T(8,128)(2,1)S(1)}, bf16[40,32,128]{2,1,0:T(8,128)(2,1)S(1)}, bf16[6,32,512]{2,1,0:T(8,128)(2,1)S(1)}, bf16[6,32,512]{2,1,0:T(8,128)(2,1)S(1)}, bf16[6,32,512]{2,1,0:T(8,128)(2,1)S(1)}) custom-call(bf16[6,32,1024]{2,1,0:T(8,128)(2,1)} %bitcast.6, bf16[6,32,1024]{2,1,0:T(8,128)(2,1)} %bitcast.7, ...), custom_call_target="tpu_custom_call" | custom-call | tf_op jit(solution)/shard_map/pack_tiles/pallas_call | solution.py:286
  1.9 7.7 %collective-permute-start = (bf16[56,32,128]{2,1,0:T(8,128)(2,1)S(1)}, bf16[56,32,128]{2,1,0:T(8,128)(2,1)S(1)}, u32[]{:S(2)}, u32[]{:S(2)}) collective-permute-start(bf16[56,32,128]{2,1,0:T(8,128)(2,1)S(1)} %get-tuple-element.16.sent_ref), channel_id=1, source_target_pairs={{0,256},{32,288},{64,320},{96,352},{128,384},{160,416},{192,448},{... | collective-permute-start | bytes 1376264 | tf_op jit(solution)/shard_map/ppermute | solution.py:260
  9.7 1.8 %pack_rows.1 = bf16[32,10,8,128]{3,2,1,0:T(8,128)(2,1)} custom-call(bf16[6,32,512]{2,1,0:T(8,128)(2,1)S(1)} %get-tuple-element.22.q_ref, bf16[6,32,512]{2,1,0:T(8,128)(2,1)S(1)} %get-tuple-element.23.k_ref, bf16[6,32,512]{2,1,0:T(8,128)(2,1)S(1)} %get-tuple-element.24.v_ref, s32[6,32]{1,0:T(8,128)} %bitcast.11), custom_call_target="tpu_custom_call" | custom-call | tf_op jit(solution)/shard_map/pack_rows/pallas_call | solution.py:294
  11.4 10.6 %all-to-all-start.1 = ((bf16[32,10,8,128]{3,2,1,0:T(8,128)(2,1)}), bf16[32,10,8,128]{3,2,1,0:T(8,128)(2,1)S(1)}, u32[]{:S(2)}, u32[]{:S(2)}) async-start(bf16[32,10,8,128]{3,2,1,0:T(8,128)(2,1)} %pack_rows.1), calls=%async_computation.1 | async-start | bytes 1310720 | tf_op jit(solution)/shard_map/all_to_all | solution.py:301
  22.1 0.1 gather_x.1
  22.2 3.4 %collective-permute-start.1 = (bf16[52,32,128]{2,1,0:T(8,128)(2,1)S(1)}, bf16[52,32,128]{2,1,0:T(8,128)(2,1)S(1)}, u32[]{:S(2)}, u32[]{:S(2)}) collective-permute-start(bf16[52,32,128]{2,1,0:T(8,128)(2,1)S(1)} %get-tuple-element.19), channel_id=1, source_target_pairs={{0,64},{32,96},{64,128},{96,160},{128,192},{160,224},{192,0},{224,... | collective-permute-start | bytes 1277960 | tf_op jit(solution)/shard_map/ppermute | solution.py:269
  25.6 3.7 %collective-permute-start.3 = (bf16[52,32,128]{2,1,0:T(8,128)(2,1)S(1)}, bf16[52,32,128]{2,1,0:T(8,128)(2,1)S(1)}, u32[]{:S(2)}, u32[]{:S(2)}) collective-permute-start(bf16[52,32,128]{2,1,0:T(8,128)(2,1)S(1)} %get-tuple-element.21), channel_id=1, source_target_pairs={{0,192},{32,224},{64,0},{96,32},{128,64},{160,96},{192,128},{224,1... | collective-permute-start | bytes 1277960 | tf_op jit(solution)/shard_map/ppermute | solution.py:269
  29.2 3.7 %collective-permute-start.2 = (bf16[20,32,128]{2,1,0:T(8,128)(2,1)S(1)}, bf16[20,32,128]{2,1,0:T(8,128)(2,1)S(1)}, u32[]{:S(2)}, u32[]{:S(2)}) collective-permute-start(bf16[20,32,128]{2,1,0:T(8,128)(2,1)S(1)} %get-tuple-element.20), channel_id=1, source_target_pairs={{0,128},{32,160},{64,192},{96,224},{128,0},{160,32},{192,64},{224,... | collective-permute-start | bytes 491528 | tf_op jit(solution)/shard_map/ppermute | solution.py:269
  33.0 7.8 %collective-permute-done.2.refs_2_ = bf16[20,32,128]{2,1,0:T(8,128)(2,1)S(1)} collective-permute-done((bf16[20,32,128]{2,1,0:T(8,128)(2,1)S(1)}, bf16[20,32,128]{2,1,0:T(8,128)(2,1)S(1)}, u32[]{:S(2)}, u32[]{:S(2)}) %collective-permute-start.2) | collective-permute-done | bytes 163872 | tf_op jit(solution)/shard_map/ppermute | solution.py:269
  40.8 0.2 collective-permute-done.3.refs_3_.right_ref
  41.0 1.9 %collective-permute-start.4 = (bf16[56,32,128]{2,1,0:T(8,128)(2,1)S(1)}, bf16[56,32,128]{2,1,0:T(8,128)(2,1)S(1)}, u32[]{:S(2)}, u32[]{:S(2)}) collective-permute-start(bf16[56,32,128]{2,1,0:T(8,128)(2,1)S(1)} %stack_keys.1), channel_id=1, source_target_pairs={{0,32},{32,0},{64,96},{96,64},{128,160},{160,128},{192,224},{224,1... | collective-permute-start | bytes 1376264 | tf_op jit(solution)/shard_map/ppermute | solution.py:264
  42.9 0.1 early_weights.1
  43.0 2.4 %collective-permute-start.5 = (bf16[96,32,128]{2,1,0:T(8,128)(2,1)S(1)}, bf16[96,32,128]{2,1,0:T(8,128)(2,1)}, u32[]{:S(2)}, u32[]{:S(2)}) collective-permute-start(bf16[96,32,128]{2,1,0:T(8,128)(2,1)S(1)} %get-tuple-element.25.early_ref), channel_id=1, source_target_pairs={{0,32},{32,0},{64,96},{96,64},{128,160},{160,128},{192,224},{224,1... | collective-permute-start | bytes 2359304 | tf_op jit(solution)/shard_map/ppermute | solution.py:264
  45.5 2.3 %attend_columns.1.after_ref = bf16[8,3,32,128]{3,2,1,0:T(8,128)(2,1)} custom-call(bf16[20,32,128]{2,1,0:T(8,128)(2,1)S(1)} %get-tuple-element.18.refs_0_, bf16[52,32,128]{2,1,0:T(8,128)(2,1)S(1)} %collective-permute-done.1.refs_1_.left_ref, bf16[20,32,128]{2,1,0:T(8,128)(2,1)S(1)} %collective-permute-done.2.refs_2_, ...), custom_call_target="tpu_custom_call" | custom-call | tf_op jit(solution)/shard_map/attend_columns/pallas_call | solution.py:320
  47.8 6.4 %all-to-all-start = ((bf16[8,3,32,128]{3,2,1,0:T(8,128)(2,1)}), bf16[8,3,32,128]{3,2,1,0:T(8,128)(2,1)S(1)}, u32[]{:S(2)}, u32[]{:S(2)}) async-start(bf16[8,3,32,128]{3,2,1,0:T(8,128)(2,1)} %attend_columns.1.after_ref), calls=%async_computation | async-start | bytes 393216 | tf_op jit(solution)/shard_map/all_to_all | solution.py:324
  54.2 3.4 %collective-permute-start.6 = (bf16[32,32,128]{2,1,0:T(8,128)(2,1)S(1)}, bf16[32,32,128]{2,1,0:T(8,128)(2,1)S(1)}, u32[]{:S(2)}, u32[]{:S(2)}) collective-permute-start(bf16[32,32,128]{2,1,0:T(8,128)(2,1)S(1)} %get-tuple-element.26), channel_id=1, source_target_pairs={{0,64},{32,96},{64,0},{96,32},{128,192},{160,224},{192,128},{224,1... | collective-permute-start | bytes 786440 | tf_op jit(solution)/shard_map/ppermute | solution.py:273
  57.5 2.8 %attend_rows.1 = bf16[32,3,8,128]{3,2,1,0:T(8,128)(2,1)} custom-call(bf16[32,10,8,128]{3,2,1,0:T(8,128)(2,1)S(1)} %all-to-all-done.1.in_ref, bf16[8,3,32,128]{3,2,1,0:T(8,128)(2,1)} %attend_columns.1.after_ref), custom_call_target="tpu_custom_call" | custom-call | tf_op jit(solution)/shard_map/attend_rows/pallas_call | solution.py:327
  60.4 11.9 %all-to-all-start.2 = ((bf16[32,3,8,128]{3,2,1,0:T(8,128)(2,1)}), bf16[32,3,8,128]{3,2,1,0:T(8,128)(2,1)S(1)}, u32[]{:S(2)}, u32[]{:S(2)}) async-start(bf16[32,3,8,128]{3,2,1,0:T(8,128)(2,1)} %attend_rows.1), calls=%async_computation.2 | async-start | bytes 393216 | tf_op jit(solution)/shard_map/all_to_all | solution.py:342
  72.3 1.9 %collective-permute-start.7 = (bf16[32,32,128]{2,1,0:T(8,128)(2,1)S(1)}, bf16[32,32,128]{2,1,0:T(8,128)(2,1)S(1)}, u32[]{:S(2)}, u32[]{:S(2)}) collective-permute-start(bf16[32,32,128]{2,1,0:T(8,128)(2,1)S(1)} %collective-permute-done.6.late_ref), channel_id=1, source_target_pairs={{0,32},{32,0},{64,96},{96,64},{128,160},{160,128},{192,224},{224,1... | collective-permute-start | bytes 786440 | tf_op jit(solution)/shard_map/ppermute | solution.py:264
  74.3 1.5 %collective-permute-done.7.late_other_ref = bf16[32,32,128]{2,1,0:T(8,128)(2,1)S(1)} collective-permute-done((bf16[32,32,128]{2,1,0:T(8,128)(2,1)S(1)}, bf16[32,32,128]{2,1,0:T(8,128)(2,1)S(1)}, u32[]{:S(2)}, u32[]{:S(2)}) %collective-permute-start.7) | collective-permute-done | bytes 262176 | tf_op jit(solution)/shard_map/ppermute | solution.py:264
  75.8 0.7 copy-done.2
  76.5 1.9 %assemble_weights.1.w_ref = bf16[1024,1024]{1,0:T(8,128)(2,1)S(1)} custom-call(bf16[96,32,128]{2,1,0:T(8,128)(2,1)} %copy-done, bf16[96,32,128]{2,1,0:T(8,128)(2,1)} %collective-permute-done.5.early_other_ref, bf16[32,32,128]{2,1,0:T(8,128)(2,1)} %copy-done.1, bf16[32,32,128]{2,1,0:T(8,128)(2,1)} %copy-done.2), custom_call_target="tpu_custom_call" | custom-call | tf_op jit(solution)/shard_map/assemble_weights/pallas_call | solution.py:339
  78.4 6.5 %all-to-all-done.2.row_ref = bf16[32,3,8,128]{3,2,1,0:T(8,128)(2,1)S(1)} async-done(((bf16[32,3,8,128]{3,2,1,0:T(8,128)(2,1)}), bf16[32,3,8,128]{3,2,1,0:T(8,128)(2,1)S(1)}, u32[]{:S(2)}, u32[]{:S(2)}) %all-to-all-start.2) | async-done | bytes 196640 | tf_op jit(solution)/shard_map/all_to_all | solution.py:342
  84.9 1.6 %project.1 = bf16[6,32,1024]{2,1,0:T(8,128)(2,1)} custom-call(bf16[8,3,32,128]{3,2,1,0:T(8,128)(2,1)S(1)} %all-to-all-done.column_ref, bf16[32,3,8,128]{3,2,1,0:T(8,128)(2,1)S(1)} %all-to-all-done.2.row_ref, bf16[1024,1024]{1,0:T(8,128)(2,1)S(1)} %assemble_weights.1.w_ref), custom_call_target="tpu_custom_call" | custom-call | tf_op jit(solution)/shard_map/project/pallas_call | solution.py:343
  (13 shorter events, 0.1 us)
Async XLA Ops:
  1.9 20.1 %collective-permute-start = (bf16[56,32,128]{2,1,0:T(8,128)(2,1)S(1)}, bf16[56,32,128]{2,1,0:T(8,128)(2,1)S(1)}, u32[]{:S(2)}, u32[]{:S(2)}) collective-permute-start(bf16[56,32,128]{2,1,0:T(8,128)(2,1)S(1)} %get-tuple-element.16.sent_ref), channel_id=1, source_target_pairs={{0,256},{32,288},{64,320},{96,352},{128,384},{160,416},{192,448},{... | collective-permute-start | bytes 1376264 | tf_op jit(solution)/shard_map/ppermute | solution.py:260
  11.4 36.3 %all-to-all-start.1 = ((bf16[32,10,8,128]{3,2,1,0:T(8,128)(2,1)}), bf16[32,10,8,128]{3,2,1,0:T(8,128)(2,1)S(1)}, u32[]{:S(2)}, u32[]{:S(2)}) async-start(bf16[32,10,8,128]{3,2,1,0:T(8,128)(2,1)} %pack_rows.1), calls=%async_computation.1 | async-start | bytes 1310720 | tf_op jit(solution)/shard_map/all_to_all | solution.py:301
  22.2 18.6 %collective-permute-start.1 = (bf16[52,32,128]{2,1,0:T(8,128)(2,1)S(1)}, bf16[52,32,128]{2,1,0:T(8,128)(2,1)S(1)}, u32[]{:S(2)}, u32[]{:S(2)}) collective-permute-start(bf16[52,32,128]{2,1,0:T(8,128)(2,1)S(1)} %get-tuple-element.19), channel_id=1, source_target_pairs={{0,64},{32,96},{64,128},{96,160},{128,192},{160,224},{192,0},{224,... | collective-permute-start | bytes 1277960 | tf_op jit(solution)/shard_map/ppermute | solution.py:269
  25.6 15.4 %collective-permute-start.3 = (bf16[52,32,128]{2,1,0:T(8,128)(2,1)S(1)}, bf16[52,32,128]{2,1,0:T(8,128)(2,1)S(1)}, u32[]{:S(2)}, u32[]{:S(2)}) collective-permute-start(bf16[52,32,128]{2,1,0:T(8,128)(2,1)S(1)} %get-tuple-element.21), channel_id=1, source_target_pairs={{0,192},{32,224},{64,0},{96,32},{128,64},{160,96},{192,128},{224,1... | collective-permute-start | bytes 1277960 | tf_op jit(solution)/shard_map/ppermute | solution.py:269
  29.2 11.5 %collective-permute-start.2 = (bf16[20,32,128]{2,1,0:T(8,128)(2,1)S(1)}, bf16[20,32,128]{2,1,0:T(8,128)(2,1)S(1)}, u32[]{:S(2)}, u32[]{:S(2)}) collective-permute-start(bf16[20,32,128]{2,1,0:T(8,128)(2,1)S(1)} %get-tuple-element.20), channel_id=1, source_target_pairs={{0,128},{32,160},{64,192},{96,224},{128,0},{160,32},{192,64},{224,... | collective-permute-start | bytes 491528 | tf_op jit(solution)/shard_map/ppermute | solution.py:269
  41.0 4.4 %collective-permute-start.4 = (bf16[56,32,128]{2,1,0:T(8,128)(2,1)S(1)}, bf16[56,32,128]{2,1,0:T(8,128)(2,1)S(1)}, u32[]{:S(2)}, u32[]{:S(2)}) collective-permute-start(bf16[56,32,128]{2,1,0:T(8,128)(2,1)S(1)} %stack_keys.1), channel_id=1, source_target_pairs={{0,32},{32,0},{64,96},{96,64},{128,160},{160,128},{192,224},{224,1... | collective-permute-start | bytes 1376264 | tf_op jit(solution)/shard_map/ppermute | solution.py:264
  43.0 32.7 %copy-start = (bf16[96,32,128]{2,1,0:T(8,128)(2,1)}, bf16[96,32,128]{2,1,0:T(8,128)(2,1)S(1)}, u32[]{:S(2)}) copy-start(bf16[96,32,128]{2,1,0:T(8,128)(2,1)S(1)} %get-tuple-element.25.early_ref) | copy-start | bytes 2359300
  43.0 32.7 %collective-permute-start.5 = (bf16[96,32,128]{2,1,0:T(8,128)(2,1)S(1)}, bf16[96,32,128]{2,1,0:T(8,128)(2,1)}, u32[]{:S(2)}, u32[]{:S(2)}) collective-permute-start(bf16[96,32,128]{2,1,0:T(8,128)(2,1)S(1)} %get-tuple-element.25.early_ref), channel_id=1, source_target_pairs={{0,32},{32,0},{64,96},{96,64},{128,160},{160,128},{192,224},{224,1... | collective-permute-start | bytes 2359304 | tf_op jit(solution)/shard_map/ppermute | solution.py:264
  47.8 12.6 %all-to-all-start = ((bf16[8,3,32,128]{3,2,1,0:T(8,128)(2,1)}), bf16[8,3,32,128]{3,2,1,0:T(8,128)(2,1)S(1)}, u32[]{:S(2)}, u32[]{:S(2)}) async-start(bf16[8,3,32,128]{3,2,1,0:T(8,128)(2,1)} %attend_columns.1.after_ref), calls=%async_computation | async-start | bytes 393216 | tf_op jit(solution)/shard_map/all_to_all | solution.py:324
  54.2 18.1 %collective-permute-start.6 = (bf16[32,32,128]{2,1,0:T(8,128)(2,1)S(1)}, bf16[32,32,128]{2,1,0:T(8,128)(2,1)S(1)}, u32[]{:S(2)}, u32[]{:S(2)}) collective-permute-start(bf16[32,32,128]{2,1,0:T(8,128)(2,1)S(1)} %get-tuple-element.26), channel_id=1, source_target_pairs={{0,64},{32,96},{64,0},{96,32},{128,192},{160,224},{192,128},{224,1... | collective-permute-start | bytes 786440 | tf_op jit(solution)/shard_map/ppermute | solution.py:273
  60.4 24.5 %all-to-all-start.2 = ((bf16[32,3,8,128]{3,2,1,0:T(8,128)(2,1)}), bf16[32,3,8,128]{3,2,1,0:T(8,128)(2,1)S(1)}, u32[]{:S(2)}, u32[]{:S(2)}) async-start(bf16[32,3,8,128]{3,2,1,0:T(8,128)(2,1)} %attend_rows.1), calls=%async_computation.2 | async-start | bytes 393216 | tf_op jit(solution)/shard_map/all_to_all | solution.py:342
  72.3 3.4 %copy-start.1 = (bf16[32,32,128]{2,1,0:T(8,128)(2,1)}, bf16[32,32,128]{2,1,0:T(8,128)(2,1)S(1)}, u32[]{:S(2)}) copy-start(bf16[32,32,128]{2,1,0:T(8,128)(2,1)S(1)} %collective-permute-done.6.late_ref) | copy-start | bytes 786436
  72.3 3.4 %collective-permute-start.7 = (bf16[32,32,128]{2,1,0:T(8,128)(2,1)S(1)}, bf16[32,32,128]{2,1,0:T(8,128)(2,1)S(1)}, u32[]{:S(2)}, u32[]{:S(2)}) collective-permute-start(bf16[32,32,128]{2,1,0:T(8,128)(2,1)S(1)} %collective-permute-done.6.late_ref), channel_id=1, source_target_pairs={{0,32},{32,0},{64,96},{96,64},{128,160},{160,128},{192,224},{224,1... | collective-permute-start | bytes 786440 | tf_op jit(solution)/shard_map/ppermute | solution.py:264
  75.8 0.7 copy-start.2

commit v3 on v2

--- a/solution.py
+++ b/solution.py
@@ -49,8 +49,12 @@
         copy.wait()
 
 
-def pack_rows_kernel(q_ref, k_ref, v_ref, m_hbm, out_ref, m_ref, sems):
-    fetch([m_hbm], [m_ref], sems)
+def place():
+    me = lax.axis_index("row")
+    return me // 8, (me // 2) % 4, me % 2
+
+
+def pack_rows(q_ref, k_ref, v_ref, m_ref, out_ref):
     bias = bias_lanes(m_ref[...], 0, 0, 6)
     low = low_lanes((6, 32, 128))
     for pair in range(HALF // 2):
@@ -74,12 +78,7 @@
                 out_ref[block, 9] = bias[rows].astype(jnp.bfloat16)
 
 
-def place():
-    me = lax.axis_index("row")
-    return me // 8, (me // 2) % 4, me % 2
-
-
-def pack_tiles_kernel(q_hbm, k_hbm, v_hbm, m_hbm, w_hbm, send_ref, keep_ref, *refs):
+def pack_kernel(q_hbm, k_hbm, v_hbm, m_hbm, w_hbm, send_ref, keep_ref, out_ref, *refs):
     (*row_refs, m_ref, sems), (y, _, _) = refs, place()
     copies = [(m_hbm, m_ref)]
     for source, target in zip((q_hbm, k_hbm, v_hbm), row_refs):
@@ -99,6 +98,7 @@
         bias = bias_lanes(m_ref[...], 3 * half, 0, 3).astype(jnp.bfloat16)
         for pair in range(4):
             ref[UNIT * pair + UNIT - 1] = bias
+    pack_rows(*row_refs, m_ref, out_ref)
 
 
 def gather_x_kernel(sent_ref, own_ref, other_ref, *out_refs):
@@ -283,21 +283,15 @@
     ]
     merges = pltpu.with_memory_space_constraint(jnp.transpose(merge_sizes), pltpu.HBM)
     w_part = pltpu.with_memory_space_constraint(jnp.transpose(w_out), pltpu.HBM)
-    sent, own, *row_halves = call(
-        pack_tiles_kernel,
-        [(4 * UNIT + W_TILES, 32, 128), (4 * UNIT, 32, 128)] + [(6, 32, WIDTH)] * 3,
-        "pack_tiles",
+    sent, own, row_packed = call(
+        pack_kernel,
+        [(4 * UNIT + W_TILES, 32, 128), (4 * UNIT, 32, 128), (32, 10, 8, 128)],
+        "pack",
         [hbm] * 5,
-        [pltpu.VMEM((6, 32), jnp.int32), pltpu.SemaphoreType.DMA((44,))],
+        [pltpu.VMEM((6, 32, WIDTH), jnp.bfloat16)] * 3
+        + [pltpu.VMEM((6, 32), jnp.int32), pltpu.SemaphoreType.DMA((44,))],
     )(*tokens, merges, w_part)
     other = across_y(sent)
-    (row_packed,) = call(
-        pack_rows_kernel,
-        [(32, 10, 8, 128)],
-        "pack_rows",
-        [vmem] * 3 + [hbm],
-        [pltpu.VMEM((6, 32), jnp.int32), pltpu.SemaphoreType.DMA((1,))],
-    )(*row_halves, merges)
     row_moved = lax.all_to_all(row_packed, "col", 0, 0, tiled=True)
     by_x = call(
         gather_x_kernel,

time: 87.2 us -> 86.3 us (0.990)
  Pallas kernels: 12.5 us -> 11.6 us
    pallas_call x2 -> x1, Pallas kernels: 3.69 us -> 2.8 us  [on_device(): call(pack_kernel, [(4 * UNIT + W_TILES, 32, 128), (4 * UNIT, 32, 128), (3...]
  transfers between devices with their start and end apart: 11 -> 11, of which waited for: 4 -> 4; matrix products, arithmetic and copies ran while one was open for 0% -> 0% of each run, Pallas kernels for 10% -> 8%
where the time goes in v3:
time: 86.3 us; the launch traced here: 85.6 us
  starting transfers between devices  57.1 us (66%)
  waiting for transfers between devices  16.1 us (19%)
  Pallas kernels  11.6 us (13%)
    all_to_all x1, starting transfers between devices, on_device(): row_back = lax.all_to_all(row_out, 'col', 0, 0, tiled=True)  11.9 us
    ppermute x3, starting transfers between devices, along_x(): return lax.ppermute(array, 'row', pairs)  10.8 us
    all_to_all x1, starting transfers between devices, on_device(): row_moved = lax.all_to_all(row_packed, 'col', 0, 0, tiled=True)  10.6 us
    ppermute x3, waiting for transfers between devices, along_x(): return lax.ppermute(array, 'row', pairs)  8.02 us
    ppermute x1, starting transfers between devices, across_y(): return lax.ppermute(array, 'row', [(i, (i + 8) % 16) for i in range(16)])  7.73 us
    all_to_all x1, waiting for transfers between devices, on_device(): row_back = lax.all_to_all(row_out, 'col', 0, 0, tiled=True)  6.53 us
    all_to_all x1, starting transfers between devices, on_device(): lax.all_to_all(column_out, 'row', 0, 0, tiled=True, axis_index_groups=SAM...  6.4 us
    ppermute x3, starting transfers between devices, across_core(): lax.ppermute(array, 'row', [(i, i // 2 * 2 + (i + 1) % 2) for i in range(...  6.25 us
  transfers between devices with their start and end apart: 11, of which 4 were waited for; matrix products, arithmetic and copies ran while one was open for 0% of the time, Pallas kernels for 8%

profile of v3, /device:TPU:8, one launch (start us, length us, event | category | flops | bytes accessed | tf_op | source)
XLA Modules:
  0.0 85.6 jit_solution(3507863290670062825)
XLA Ops:
  0.0 2.8 %pack.1 = (bf16[56,32,128]{2,1,0:T(8,128)(2,1)S(1)}, bf16[40,32,128]{2,1,0:T(8,128)(2,1)S(1)}, bf16[32,10,8,128]{3,2,1,0:T(8,128)(2,1)}) custom-call(bf16[6,32,1024]{2,1,0:T(8,128)(2,1)} %bitcast.6, bf16[6,32,1024]{2,1,0:T(8,128)(2,1)} %bitcast.7, bf16[6,32,1024]{2,1,0:T(8,128)(2,1)} %bitcast.8, s32[6,32]{1,0:T(8,128)} %bitcast.10, bf16[64,1024]{1,0:T(8,128)(2,1)} %bitcast.9), custom_call_target="tpu_custom_call" | custom-call | tf_op jit(solution)/shard_map/pack/pallas_call | solution.py:286
  2.8 7.7 %collective-permute-start = (bf16[56,32,128]{2,1,0:T(8,128)(2,1)S(1)}, bf16[56,32,128]{2,1,0:T(8,128)(2,1)S(1)}, u32[]{:S(2)}, u32[]{:S(2)}) collective-permute-start(bf16[56,32,128]{2,1,0:T(8,128)(2,1)S(1)} %get-tuple-element.14.sent_ref), channel_id=1, source_target_pairs={{0,256},{32,288},{64,320},{96,352},{128,384},{160,416},{192,448},{... | collective-permute-start | bytes 1376264 | tf_op jit(solution)/shard_map/ppermute | solution.py:260
  10.5 10.6 %all-to-all-start.1 = ((bf16[32,10,8,128]{3,2,1,0:T(8,128)(2,1)}), bf16[32,10,8,128]{3,2,1,0:T(8,128)(2,1)S(1)}, u32[]{:S(2)}, u32[]{:S(2)}) async-start(bf16[32,10,8,128]{3,2,1,0:T(8,128)(2,1)} %get-tuple-element.20), calls=%async_computation.1 | async-start | bytes 1310720 | tf_op jit(solution)/shard_map/all_to_all | solution.py:295
  21.2 0.1 gather_x.1
  21.3 3.4 %collective-permute-start.1 = (bf16[52,32,128]{2,1,0:T(8,128)(2,1)S(1)}, bf16[52,32,128]{2,1,0:T(8,128)(2,1)S(1)}, u32[]{:S(2)}, u32[]{:S(2)}) collective-permute-start(bf16[52,32,128]{2,1,0:T(8,128)(2,1)S(1)} %get-tuple-element.17), channel_id=1, source_target_pairs={{0,64},{32,96},{64,128},{96,160},{128,192},{160,224},{192,0},{224,... | collective-permute-start | bytes 1277960 | tf_op jit(solution)/shard_map/ppermute | solution.py:269
  24.7 3.7 %collective-permute-start.3 = (bf16[52,32,128]{2,1,0:T(8,128)(2,1)S(1)}, bf16[52,32,128]{2,1,0:T(8,128)(2,1)S(1)}, u32[]{:S(2)}, u32[]{:S(2)}) collective-permute-start(bf16[52,32,128]{2,1,0:T(8,128)(2,1)S(1)} %get-tuple-element.19), channel_id=1, source_target_pairs={{0,192},{32,224},{64,0},{96,32},{128,64},{160,96},{192,128},{224,1... | collective-permute-start | bytes 1277960 | tf_op jit(solution)/shard_map/ppermute | solution.py:269
  28.3 3.7 %collective-permute-start.2 = (bf16[20,32,128]{2,1,0:T(8,128)(2,1)S(1)}, bf16[20,32,128]{2,1,0:T(8,128)(2,1)S(1)}, u32[]{:S(2)}, u32[]{:S(2)}) collective-permute-start(bf16[20,32,128]{2,1,0:T(8,128)(2,1)S(1)} %get-tuple-element.18), channel_id=1, source_target_pairs={{0,128},{32,160},{64,192},{96,224},{128,0},{160,32},{192,64},{224,... | collective-permute-start | bytes 491528 | tf_op jit(solution)/shard_map/ppermute | solution.py:269
  32.1 7.8 %collective-permute-done.2.refs_2_ = bf16[20,32,128]{2,1,0:T(8,128)(2,1)S(1)} collective-permute-done((bf16[20,32,128]{2,1,0:T(8,128)(2,1)S(1)}, bf16[20,32,128]{2,1,0:T(8,128)(2,1)S(1)}, u32[]{:S(2)}, u32[]{:S(2)}) %collective-permute-start.2) | collective-permute-done | bytes 163872 | tf_op jit(solution)/shard_map/ppermute | solution.py:269
  39.9 0.2 collective-permute-done.3.refs_3_.right_ref
  40.1 1.9 %collective-permute-start.4 = (bf16[56,32,128]{2,1,0:T(8,128)(2,1)S(1)}, bf16[56,32,128]{2,1,0:T(8,128)(2,1)S(1)}, u32[]{:S(2)}, u32[]{:S(2)}) collective-permute-start(bf16[56,32,128]{2,1,0:T(8,128)(2,1)S(1)} %stack_keys.1), channel_id=1, source_target_pairs={{0,32},{32,0},{64,96},{96,64},{128,160},{160,128},{192,224},{224,1... | collective-permute-start | bytes 1376264 | tf_op jit(solution)/shard_map/ppermute | solution.py:264
  42.0 0.1 early_weights.1
  42.1 2.4 %collective-permute-start.5 = (bf16[96,32,128]{2,1,0:T(8,128)(2,1)S(1)}, bf16[96,32,128]{2,1,0:T(8,128)(2,1)}, u32[]{:S(2)}, u32[]{:S(2)}) collective-permute-start(bf16[96,32,128]{2,1,0:T(8,128)(2,1)S(1)} %get-tuple-element.21.early_ref), channel_id=1, source_target_pairs={{0,32},{32,0},{64,96},{96,64},{128,160},{160,128},{192,224},{224,1... | collective-permute-start | bytes 2359304 | tf_op jit(solution)/shard_map/ppermute | solution.py:264
  44.6 2.3 %attend_columns.1.after_ref = bf16[8,3,32,128]{3,2,1,0:T(8,128)(2,1)} custom-call(bf16[20,32,128]{2,1,0:T(8,128)(2,1)S(1)} %get-tuple-element.16.refs_0_, bf16[52,32,128]{2,1,0:T(8,128)(2,1)S(1)} %collective-permute-done.1.refs_1_.left_ref, bf16[20,32,128]{2,1,0:T(8,128)(2,1)S(1)} %collective-permute-done.2.refs_2_, ...), custom_call_target="tpu_custom_call" | custom-call | tf_op jit(solution)/shard_map/attend_columns/pallas_call | solution.py:314
  46.9 6.4 %all-to-all-start = ((bf16[8,3,32,128]{3,2,1,0:T(8,128)(2,1)}), bf16[8,3,32,128]{3,2,1,0:T(8,128)(2,1)S(1)}, u32[]{:S(2)}, u32[]{:S(2)}) async-start(bf16[8,3,32,128]{3,2,1,0:T(8,128)(2,1)} %attend_columns.1.after_ref), calls=%async_computation | async-start | bytes 393216 | tf_op jit(solution)/shard_map/all_to_all | solution.py:318
  53.3 3.4 %collective-permute-start.6 = (bf16[32,32,128]{2,1,0:T(8,128)(2,1)S(1)}, bf16[32,32,128]{2,1,0:T(8,128)(2,1)S(1)}, u32[]{:S(2)}, u32[]{:S(2)}) collective-permute-start(bf16[32,32,128]{2,1,0:T(8,128)(2,1)S(1)} %get-tuple-element.22), channel_id=1, source_target_pairs={{0,64},{32,96},{64,0},{96,32},{128,192},{160,224},{192,128},{224,1... | collective-permute-start | bytes 786440 | tf_op jit(solution)/shard_map/ppermute | solution.py:273
  56.7 2.8 %attend_rows.1 = bf16[32,3,8,128]{3,2,1,0:T(8,128)(2,1)} custom-call(bf16[32,10,8,128]{3,2,1,0:T(8,128)(2,1)S(1)} %all-to-all-done.1.in_ref, bf16[8,3,32,128]{3,2,1,0:T(8,128)(2,1)} %attend_columns.1.after_ref), custom_call_target="tpu_custom_call" | custom-call | tf_op jit(solution)/shard_map/attend_rows/pallas_call | solution.py:321
  59.5 11.9 %all-to-all-start.2 = ((bf16[32,3,8,128]{3,2,1,0:T(8,128)(2,1)}), bf16[32,3,8,128]{3,2,1,0:T(8,128)(2,1)S(1)}, u32[]{:S(2)}, u32[]{:S(2)}) async-start(bf16[32,3,8,128]{3,2,1,0:T(8,128)(2,1)} %attend_rows.1), calls=%async_computation.2 | async-start | bytes 393216 | tf_op jit(solution)/shard_map/all_to_all | solution.py:336
  71.5 0.0 copy-start.1
  71.5 1.9 %collective-permute-start.7 = (bf16[32,32,128]{2,1,0:T(8,128)(2,1)S(1)}, bf16[32,32,128]{2,1,0:T(8,128)(2,1)S(1)}, u32[]{:S(2)}, u32[]{:S(2)}) collective-permute-start(bf16[32,32,128]{2,1,0:T(8,128)(2,1)S(1)} %collective-permute-done.6.late_ref), channel_id=1, source_target_pairs={{0,32},{32,0},{64,96},{96,64},{128,160},{160,128},{192,224},{224,1... | collective-permute-start | bytes 786440 | tf_op jit(solution)/shard_map/ppermute | solution.py:264
  73.4 1.5 %collective-permute-done.7.late_other_ref = bf16[32,32,128]{2,1,0:T(8,128)(2,1)S(1)} collective-permute-done((bf16[32,32,128]{2,1,0:T(8,128)(2,1)S(1)}, bf16[32,32,128]{2,1,0:T(8,128)(2,1)S(1)}, u32[]{:S(2)}, u32[]{:S(2)}) %collective-permute-start.7) | collective-permute-done | bytes 262176 | tf_op jit(solution)/shard_map/ppermute | solution.py:264
  74.9 0.7 copy-done.2
  75.6 1.9 %assemble_weights.1.w_ref = bf16[1024,1024]{1,0:T(8,128)(2,1)S(1)} custom-call(bf16[96,32,128]{2,1,0:T(8,128)(2,1)} %copy-done, bf16[96,32,128]{2,1,0:T(8,128)(2,1)} %collective-permute-done.5.early_other_ref, bf16[32,32,128]{2,1,0:T(8,128)(2,1)} %copy-done.1, bf16[32,32,128]{2,1,0:T(8,128)(2,1)} %copy-done.2), custom_call_target="tpu_custom_call" | custom-call | tf_op jit(solution)/shard_map/assemble_weights/pallas_call | solution.py:333
  77.5 6.5 %all-to-all-done.2.row_ref = bf16[32,3,8,128]{3,2,1,0:T(8,128)(2,1)S(1)} async-done(((bf16[32,3,8,128]{3,2,1,0:T(8,128)(2,1)}), bf16[32,3,8,128]{3,2,1,0:T(8,128)(2,1)S(1)}, u32[]{:S(2)}, u32[]{:S(2)}) %all-to-all-start.2) | async-done | bytes 196640 | tf_op jit(solution)/shard_map/all_to_all | solution.py:336
  84.1 1.6 %project.1 = bf16[6,32,1024]{2,1,0:T(8,128)(2,1)} custom-call(bf16[8,3,32,128]{3,2,1,0:T(8,128)(2,1)S(1)} %all-to-all-done.column_ref, bf16[32,3,8,128]{3,2,1,0:T(8,128)(2,1)S(1)} %all-to-all-done.2.row_ref, bf16[1024,1024]{1,0:T(8,128)(2,1)S(1)} %assemble_weights.1.w_ref), custom_call_target="tpu_custom_call" | custom-call | tf_op jit(solution)/shard_map/project/pallas_call | solution.py:337
  (12 shorter events, 0.1 us)
Async XLA Ops:
  2.8 18.4 %collective-permute-start = (bf16[56,32,128]{2,1,0:T(8,128)(2,1)S(1)}, bf16[56,32,128]{2,1,0:T(8,128)(2,1)S(1)}, u32[]{:S(2)}, u32[]{:S(2)}) collective-permute-start(bf16[56,32,128]{2,1,0:T(8,128)(2,1)S(1)} %get-tuple-element.14.sent_ref), channel_id=1, source_target_pairs={{0,256},{32,288},{64,320},{96,352},{128,384},{160,416},{192,448},{... | collective-permute-start | bytes 1376264 | tf_op jit(solution)/shard_map/ppermute | solution.py:260
  10.5 36.3 %all-to-all-start.1 = ((bf16[32,10,8,128]{3,2,1,0:T(8,128)(2,1)}), bf16[32,10,8,128]{3,2,1,0:T(8,128)(2,1)S(1)}, u32[]{:S(2)}, u32[]{:S(2)}) async-start(bf16[32,10,8,128]{3,2,1,0:T(8,128)(2,1)} %get-tuple-element.20), calls=%async_computation.1 | async-start | bytes 1310720 | tf_op jit(solution)/shard_map/all_to_all | solution.py:295
  21.3 18.6 %collective-permute-start.1 = (bf16[52,32,128]{2,1,0:T(8,128)(2,1)S(1)}, bf16[52,32,128]{2,1,0:T(8,128)(2,1)S(1)}, u32[]{:S(2)}, u32[]{:S(2)}) collective-permute-start(bf16[52,32,128]{2,1,0:T(8,128)(2,1)S(1)} %get-tuple-element.17), channel_id=1, source_target_pairs={{0,64},{32,96},{64,128},{96,160},{128,192},{160,224},{192,0},{224,... | collective-permute-start | bytes 1277960 | tf_op jit(solution)/shard_map/ppermute | solution.py:269
  24.7 15.4 %collective-permute-start.3 = (bf16[52,32,128]{2,1,0:T(8,128)(2,1)S(1)}, bf16[52,32,128]{2,1,0:T(8,128)(2,1)S(1)}, u32[]{:S(2)}, u32[]{:S(2)}) collective-permute-start(bf16[52,32,128]{2,1,0:T(8,128)(2,1)S(1)} %get-tuple-element.19), channel_id=1, source_target_pairs={{0,192},{32,224},{64,0},{96,32},{128,64},{160,96},{192,128},{224,1... | collective-permute-start | bytes 1277960 | tf_op jit(solution)/shard_map/ppermute | solution.py:269
  28.3 11.5 %collective-permute-start.2 = (bf16[20,32,128]{2,1,0:T(8,128)(2,1)S(1)}, bf16[20,32,128]{2,1,0:T(8,128)(2,1)S(1)}, u32[]{:S(2)}, u32[]{:S(2)}) collective-permute-start(bf16[20,32,128]{2,1,0:T(8,128)(2,1)S(1)} %get-tuple-element.18), channel_id=1, source_target_pairs={{0,128},{32,160},{64,192},{96,224},{128,0},{160,32},{192,64},{224,... | collective-permute-start | bytes 491528 | tf_op jit(solution)/shard_map/ppermute | solution.py:269
  40.1 4.4 %collective-permute-start.4 = (bf16[56,32,128]{2,1,0:T(8,128)(2,1)S(1)}, bf16[56,32,128]{2,1,0:T(8,128)(2,1)S(1)}, u32[]{:S(2)}, u32[]{:S(2)}) collective-permute-start(bf16[56,32,128]{2,1,0:T(8,128)(2,1)S(1)} %stack_keys.1), channel_id=1, source_target_pairs={{0,32},{32,0},{64,96},{96,64},{128,160},{160,128},{192,224},{224,1... | collective-permute-start | bytes 1376264 | tf_op jit(solution)/shard_map/ppermute | solution.py:264
  42.1 32.8 %copy-start = (bf16[96,32,128]{2,1,0:T(8,128)(2,1)}, bf16[96,32,128]{2,1,0:T(8,128)(2,1)S(1)}, u32[]{:S(2)}) copy-start(bf16[96,32,128]{2,1,0:T(8,128)(2,1)S(1)} %get-tuple-element.21.early_ref) | copy-start | bytes 2359300
  42.1 32.8 %collective-permute-start.5 = (bf16[96,32,128]{2,1,0:T(8,128)(2,1)S(1)}, bf16[96,32,128]{2,1,0:T(8,128)(2,1)}, u32[]{:S(2)}, u32[]{:S(2)}) collective-permute-start(bf16[96,32,128]{2,1,0:T(8,128)(2,1)S(1)} %get-tuple-element.21.early_ref), channel_id=1, source_target_pairs={{0,32},{32,0},{64,96},{96,64},{128,160},{160,128},{192,224},{224,1... | collective-permute-start | bytes 2359304 | tf_op jit(solution)/shard_map/ppermute | solution.py:264
  46.9 12.6 %all-to-all-start = ((bf16[8,3,32,128]{3,2,1,0:T(8,128)(2,1)}), bf16[8,3,32,128]{3,2,1,0:T(8,128)(2,1)S(1)}, u32[]{:S(2)}, u32[]{:S(2)}) async-start(bf16[8,3,32,128]{3,2,1,0:T(8,128)(2,1)} %attend_columns.1.after_ref), calls=%async_computation | async-start | bytes 393216 | tf_op jit(solution)/shard_map/all_to_all | solution.py:318
  53.3 18.2 %collective-permute-start.6 = (bf16[32,32,128]{2,1,0:T(8,128)(2,1)S(1)}, bf16[32,32,128]{2,1,0:T(8,128)(2,1)S(1)}, u32[]{:S(2)}, u32[]{:S(2)}) collective-permute-start(bf16[32,32,128]{2,1,0:T(8,128)(2,1)S(1)} %get-tuple-element.22), channel_id=1, source_target_pairs={{0,64},{32,96},{64,0},{96,32},{128,192},{160,224},{192,128},{224,1... | collective-permute-start | bytes 786440 | tf_op jit(solution)/shard_map/ppermute | solution.py:273
  59.5 24.6 %all-to-all-start.2 = ((bf16[32,3,8,128]{3,2,1,0:T(8,128)(2,1)}), bf16[32,3,8,128]{3,2,1,0:T(8,128)(2,1)S(1)}, u32[]{:S(2)}, u32[]{:S(2)}) async-start(bf16[32,3,8,128]{3,2,1,0:T(8,128)(2,1)} %attend_rows.1), calls=%async_computation.2 | async-start | bytes 393216 | tf_op jit(solution)/shard_map/all_to_all | solution.py:336
  71.5 3.4 %copy-start.1 = (bf16[32,32,128]{2,1,0:T(8,128)(2,1)}, bf16[32,32,128]{2,1,0:T(8,128)(2,1)S(1)}, u32[]{:S(2)}) copy-start(bf16[32,32,128]{2,1,0:T(8,128)(2,1)S(1)} %collective-permute-done.6.late_ref) | copy-start | bytes 786436
  71.5 3.4 %collective-permute-start.7 = (bf16[32,32,128]{2,1,0:T(8,128)(2,1)S(1)}, bf16[32,32,128]{2,1,0:T(8,128)(2,1)S(1)}, u32[]{:S(2)}, u32[]{:S(2)}) collective-permute-start(bf16[32,32,128]{2,1,0:T(8,128)(2,1)S(1)} %collective-permute-done.6.late_ref), channel_id=1, source_target_pairs={{0,32},{32,0},{64,96},{96,64},{128,160},{160,128},{192,224},{224,1... | collective-permute-start | bytes 786440 | tf_op jit(solution)/shard_map/ppermute | solution.py:264
  74.9 0.7 copy-start.2

commit v4 on v3

--- a/solution.py
+++ b/solution.py
@@ -10,6 +10,8 @@
 HALF = HEADS // 2
 WIDTH = HALF * HEAD
 UNIT = 10
+X_TILES = 19
+CORE_TILES = 13
 W_TILES = 16
 SAME_CORE = [list(range(core, 16, 2)) for core in range(2)]
 LOG2E = 1.4426950408889634
@@ -38,14 +40,15 @@
     )
 
 
-def fetch(sources, targets, sems):
-    copies = [
-        pltpu.make_async_copy(source, target, sems.at[n])
-        for n, (source, target) in enumerate(zip(sources, targets))
-    ]
-    for copy in copies:
+def start(copies, sems, first=0):
+    started = [pltpu.make_async_copy(*copy, sems.at[first + n]) for n, copy in enumerate(copies)]
+    for copy in started:
         copy.start()
-    for copy in copies:
+    return started
+
+
+def wait(started):
+    for copy in started:
         copy.wait()
 
 
@@ -54,7 +57,8 @@
     return me // 8, (me // 2) % 4, me % 2
 
 
-def pack_rows(q_ref, k_ref, v_ref, m_ref, out_ref):
+def pack_rows(q_ref, k_ref, v_ref, m_ref, out_ref, out_hbm, sems):
+    outgoing = []
     bias = bias_lanes(m_ref[...], 0, 0, 6)
     low = low_lanes((6, 32, 128))
     for pair in range(HALF // 2):
@@ -72,14 +76,17 @@
             )
             for rg in range(4):
                 rows = slice(8 * rg, 8 * rg + 8)
-                block = rg * 8 + 2 * pair + odd
-                out_ref[block, 0:6] = qk[:, rows].astype(jnp.bfloat16)
-                out_ref[block, 6:9] = vv[:, rows].astype(jnp.bfloat16)
-                out_ref[block, 9] = bias[rows].astype(jnp.bfloat16)
-
-
-def pack_kernel(q_hbm, k_hbm, v_hbm, m_hbm, w_hbm, send_ref, keep_ref, out_ref, *refs):
-    (*row_refs, m_ref, sems), (y, _, _) = refs, place()
+                h = 2 * pair + odd
+                out_ref[rg, h, 0:6] = qk[:, rows].astype(jnp.bfloat16)
+                out_ref[rg, h, 6:9] = vv[:, rows].astype(jnp.bfloat16)
+                out_ref[rg, h, 9] = bias[rows].astype(jnp.bfloat16)
+        heads = pl.ds(2 * pair, 2)
+        outgoing += start([(out_ref.at[:, heads], out_hbm.at[:, heads])], sems, pair)
+    return outgoing
+
+
+def pack_kernel(q_hbm, k_hbm, v_hbm, m_hbm, w_hbm, send_ref, keep_ref, out_hbm, *refs):
+    (*row_refs, m_ref, sems, out_ref, out_sems), (y, _, _) = refs, place()
     copies = [(m_hbm, m_ref)]
     for source, target in zip((q_hbm, k_hbm, v_hbm), row_refs):
         copies.append((source.at[:, :, pl.ds(WIDTH, WIDTH)], target))
@@ -93,39 +100,48 @@
     for n in range(W_TILES):
         rows, lanes = pl.ds(n % 2 * 32, 32), pl.ds(n // 2 * 128, 128)
         copies.append((w_hbm.at[rows, lanes], send_ref.at[4 * UNIT + n]))
-    fetch(*zip(*copies), sems)
+    copies = start(copies, sems)
+    wait(copies[:4])
+    outgoing = pack_rows(*row_refs, m_ref, out_ref, out_hbm, out_sems)
+    wait(copies[4:])
     for ref, half in ((send_ref, 1 - y), (keep_ref, y)):
         bias = bias_lanes(m_ref[...], 3 * half, 0, 3).astype(jnp.bfloat16)
         for pair in range(4):
             ref[UNIT * pair + UNIT - 1] = bias
-    pack_rows(*row_refs, m_ref, out_ref)
+    wait(outgoing)
+
+
+def shift_lanes(tile, shift):
+    return pltpu.roll(tile.astype(jnp.float32), shift, 1)
 
 
 def gather_x_kernel(sent_ref, own_ref, other_ref, *out_refs):
     _, x, _ = place()
+    bias = own_ref[UNIT - 1].astype(jnp.float32) + shift_lanes(other_ref[UNIT - 1], 3)
     for dx, out_ref in enumerate(out_refs):
-        pair = pl.ds((x + dx) % 4 * UNIT, UNIT)
-        out_ref[0:UNIT] = own_ref[pair]
-        out_ref[UNIT : 2 * UNIT] = other_ref[pair]
+        pair = pl.ds((x + dx) % 4 * UNIT, 9)
+        out_ref[0:9] = own_ref[pair]
+        out_ref[9:18] = other_ref[pair]
+        out_ref[18] = bias.astype(jnp.bfloat16)
         if dx % 2:
-            out_ref[2 * UNIT : 2 * UNIT + W_TILES] = sent_ref[4 * UNIT :]
-            out_ref[2 * UNIT + W_TILES :] = other_ref[4 * UNIT :]
+            out_ref[X_TILES : X_TILES + W_TILES] = sent_ref[4 * UNIT :]
+            out_ref[X_TILES + W_TILES :] = other_ref[4 * UNIT :]
 
 
 def early_weights_kernel(sent_ref, other_ref, left_ref, right_ref, early_ref, lack_ref):
     _, x, _ = place()
     early_ref[0:W_TILES] = sent_ref[4 * UNIT :]
     early_ref[W_TILES : 2 * W_TILES] = other_ref[4 * UNIT :]
-    early_ref[2 * W_TILES : 4 * W_TILES] = left_ref[2 * UNIT :]
-    early_ref[4 * W_TILES :] = right_ref[2 * UNIT :]
+    early_ref[2 * W_TILES : 4 * W_TILES] = left_ref[X_TILES:]
+    early_ref[4 * W_TILES :] = right_ref[X_TILES:]
     lack_ref[...] = early_ref[pl.ds((2 + 2 * (x % 2)) * W_TILES, 2 * W_TILES)]
 
 
 def stack_keys_kernel(*refs):
     for dx in range(4):
-        for s in range(2):
-            first = 14 * dx + 7 * s
-            refs[4][first : first + 7] = refs[dx][UNIT * s + 3 : UNIT * s + UNIT]
+        first = CORE_TILES * dx
+        refs[4][first : first + 6] = refs[dx][3:9]
+        refs[4][first + 6 : first + 13] = refs[dx][12:19]
 
 
 def assemble_weights_kernel(early_ref, early_other_ref, late_ref, late_other_ref, w_ref):
@@ -157,7 +173,7 @@
     return summed / totals
 
 
-def attend_rows_kernel(in_ref, after_ref, out_ref, qk_ref, v_ref, b_ref, o_ref):
+def attend_rows_kernel(in_ref, after_ref, out_hbm, qk_ref, v_ref, b_ref, o_ref, out_ref, sems):
     for t in range(6):
         qk_ref[t * 256 : t * 256 + 256] = (
             in_ref[:, t].astype(jnp.float32).reshape(256, 128)
@@ -176,26 +192,32 @@
         out = attend(qk[:, :HEAD], qk[:, HEAD:], v, bias)
         out = out.T
         o_ref[pl.ds(r, 96, stride=8), :] = jnp.concatenate([out[:96], out[96:]], axis=1)
+    outgoing = []
     for j in range(3):
         out_ref[:, j] = (
             o_ref[j * 256 : j * 256 + 256].reshape(32, 8, 128).astype(jnp.bfloat16)
         )
+        outgoing += start([(out_ref.at[:, j], out_hbm.at[:, j])], sems, j)
+    wait(outgoing)
 
 
 def attend_columns_kernel(*refs):
-    in_refs, other_ref, out_ref = refs[:4], refs[4], refs[5]
+    in_refs, (other_ref, out_hbm, out_ref, sems) = refs[:4], refs[4:]
+    outgoing = []
     y, x, _ = place()
     sources = [(dx, s) for dx in range(4) for s in range(2)]
 
     def keys_of(n):
-        tiles = [in_refs[dx][UNIT * s + 3 + n] for dx, s in sources]
-        tiles += [other_ref[14 * dx + 7 * s + n] for dx, s in sources]
+        tiles = [in_refs[dx][9 * s + 3 + n] for dx, s in sources]
+        tiles += [other_ref[CORE_TILES * dx + 6 * s + n] for dx, s in sources]
         return jnp.concatenate(tiles, axis=0)
 
-    biases = keys_of(6).astype(jnp.float32) * LOG2E
+    biases = [ref[18] for ref in in_refs] + [other_ref[CORE_TILES * dx + 12] for dx in range(4)]
+    biases = [shift_lanes(tile, 125 * s % 128) for tile in biases for s in range(2)]
+    biases = jnp.concatenate(biases, axis=0) * LOG2E
     low = low_lanes((256, 128))
     for j in range(3):
-        q = jnp.concatenate([in_refs[dx][UNIT * s + j] for dx, s in sources], axis=0)
+        q = jnp.concatenate([in_refs[dx][9 * s + j] for dx, s in sources], axis=0)
         zero = jnp.zeros_like(q)
         q = jnp.concatenate([jnp.where(low, q, zero), jnp.where(low, zero, q)], axis=0)
         scores = lax.dot_general(
@@ -215,9 +237,11 @@
         out = out.astype(jnp.bfloat16)
         for n, (dx, s) in enumerate(sources):
             out_ref[(y + s) % 2 * 4 + (x - dx + 4) % 4, j] = out[32 * n : 32 * n + 32]
-
-
-def project_kernel(column_ref, row_ref, w_ref, out_ref, joined_ref):
+        outgoing += start([(out_ref.at[:, j], out_hbm.at[:, j])], sems, j)
+    wait(outgoing)
+
+
+def project_kernel(column_ref, row_ref, w_ref, out_hbm, joined_ref, out_ref, sems):
     for block in range(8):
         lanes = slice(block % 4 * 128, block % 4 * 128 + 128)
         joined_ref[block // 4 * 3 : block // 4 * 3 + 3, :, lanes] = column_ref[block]
@@ -233,23 +257,26 @@
             rows = slice(16 * half, 16 * half + 16)
             joined_ref[0:3, rows, lanes] = jnp.where(low, even, swap_halves(odd)).astype(jnp.bfloat16)
             joined_ref[3:6, rows, lanes] = jnp.where(low, swap_halves(even), odd).astype(jnp.bfloat16)
-    mixed = lax.dot_general(
-        joined_ref[...].reshape(192, 2 * WIDTH),
-        w_ref[...],
-        (((1,), (1,)), ((), ())),
-        preferred_element_type=jnp.float32,
-    )
-    out_ref[...] = mixed.astype(jnp.bfloat16).reshape(6, 32, 2 * WIDTH)
-
-
-def call(kernel, out_shapes, name, in_specs, scratch=()):
+    joined = joined_ref[...].reshape(192, 2 * WIDTH)
+    outgoing = []
+    for n in range(4):
+        lanes = pl.ds(256 * n, 256)
+        mixed = lax.dot_general(
+            joined, w_ref[lanes], (((1,), (1,)), ((), ())), preferred_element_type=jnp.float32
+        )
+        out_ref[:, :, lanes] = mixed.astype(jnp.bfloat16).reshape(6, 32, 256)
+        outgoing += start([(out_ref.at[:, :, lanes], out_hbm.at[:, :, lanes])], sems, n)
+    wait(outgoing)
+
+
+def call(kernel, out_shapes, name, in_specs, scratch=(), out_specs=None):
     vmem = pl.BlockSpec(memory_space=pltpu.VMEM)
     shapes = [jax.ShapeDtypeStruct(shape, jnp.bfloat16) for shape in out_shapes]
     return pl.pallas_call(
         kernel,
         out_shape=shapes,
         in_specs=in_specs,
-        out_specs=[vmem] * len(shapes),
+        out_specs=out_specs or [vmem] * len(shapes),
         scratch_shapes=list(scratch),
         compiler_params=pltpu.CompilerParams(vmem_limit_bytes=VMEM_LIMIT),
         name=name,
@@ -285,22 +312,24 @@
     w_part = pltpu.with_memory_space_constraint(jnp.transpose(w_out), pltpu.HBM)
     sent, own, row_packed = call(
         pack_kernel,
-        [(4 * UNIT + W_TILES, 32, 128), (4 * UNIT, 32, 128), (32, 10, 8, 128)],
+        [(4 * UNIT + W_TILES, 32, 128), (4 * UNIT, 32, 128), (4, 8, 10, 8, 128)],
         "pack",
         [hbm] * 5,
         [pltpu.VMEM((6, 32, WIDTH), jnp.bfloat16)] * 3
-        + [pltpu.VMEM((6, 32), jnp.int32), pltpu.SemaphoreType.DMA((44,))],
+        + [pltpu.VMEM((6, 32), jnp.int32), pltpu.SemaphoreType.DMA((44,))]
+        + [pltpu.VMEM((4, 8, 10, 8, 128), jnp.bfloat16), pltpu.SemaphoreType.DMA((4,))],
+        [vmem, vmem, hbm],
     )(*tokens, merges, w_part)
     other = across_y(sent)
-    row_moved = lax.all_to_all(row_packed, "col", 0, 0, tiled=True)
+    row_moved = lax.all_to_all(row_packed.reshape(32, 10, 8, 128), "col", 0, 0, tiled=True)
     by_x = call(
         gather_x_kernel,
-        [(2 * UNIT + dx % 2 * 2 * W_TILES, 32, 128) for dx in range(4)],
+        [(X_TILES + dx % 2 * 2 * W_TILES, 32, 128) for dx in range(4)],
         "gather_x",
         [vmem] * 3,
     )(sent, own, other)
     by_x = [by_x[0]] + [along_x(by_x[dx], dx) for dx in (1, 2, 3)]
-    (keys,) = call(stack_keys_kernel, [(56, 32, 128)], "stack_keys", [vmem] * 4)(*by_x)
+    (keys,) = call(stack_keys_kernel, [(4 * CORE_TILES, 32, 128)], "stack_keys", [vmem] * 4)(*by_x)
     other_keys = across_core(keys)
     early, lack = call(
         early_weights_kernel,
@@ -311,9 +340,14 @@
     late = swap_x(lack)
     weights = [early, across_core(early), late, across_core(late)]
     weights = [pltpu.with_memory_space_constraint(x, pltpu.HBM) for x in weights]
-    (column_out,) = call(attend_columns_kernel, [(8, 3, 32, 128)], "attend_columns", [vmem] * 5)(
-        *by_x, other_keys
-    )
+    (column_out,) = call(
+        attend_columns_kernel,
+        [(8, 3, 32, 128)],
+        "attend_columns",
+        [vmem] * 5,
+        [pltpu.VMEM((8, 3, 32, 128), jnp.bfloat16), pltpu.SemaphoreType.DMA((3,))],
+        [hbm],
+    )(*by_x, other_keys)
     column_done = column_out
     column_out = lax.all_to_all(
         column_out, "row", 0, 0, tiled=True, axis_index_groups=SAME_CORE
@@ -328,7 +362,10 @@
             pltpu.VMEM((768, 128), jnp.float32),
             pltpu.VMEM((256, 128), jnp.float32),
             pltpu.VMEM((768, 128), jnp.float32),
+            pltpu.VMEM((32, 3, 8, 128), jnp.bfloat16),
+            pltpu.SemaphoreType.DMA((3,)),
         ],
+        [hbm],
     )(row_moved, column_done)
     (weights,) = call(
         assemble_weights_kernel, [(2 * WIDTH, 2 * WIDTH)], "assemble_weights", [vmem] * 4
@@ -339,7 +376,8 @@
         [(6, 32, 2 * WIDTH)],
         "project",
         [vmem] * 3,
-        [pltpu.VMEM((6, 32, 2 * WIDTH), jnp.bfloat16)],
+        [pltpu.VMEM((6, 32, 2 * WIDTH), jnp.bfloat16)] * 2 + [pltpu.SemaphoreType.DMA((4,))],
+        [hbm],
     )(column_out, row_back, weights)
     return jnp.swapaxes(mixed, 0, 1)
 

time: 86.3 us -> 85.8 us (level)
  transfers between devices with their start and end apart: 11 -> 11, of which waited for: 4 -> 4; matrix products, arithmetic and copies ran while one was open for 0% -> 0% of each run, Pallas kernels for 8% -> 9%
where the time goes in v4:
time: 85.8 us; the launch traced here: 85.2 us
  starting transfers between devices  57.1 us (67%)
  waiting for transfers between devices  15.7 us (18%)
  Pallas kernels  11.5 us (13%)
    all_to_all x1, starting transfers between devices, on_device(): row_back = lax.all_to_all(row_out, 'col', 0, 0, tiled=True)  12 us
    ppermute x3, starting transfers between devices, along_x(): return lax.ppermute(array, 'row', pairs)  10.8 us
    all_to_all x1, starting transfers between devices, on_device(): lax.all_to_all(row_packed.reshape(32, 10, 8, 128), 'col', 0, 0, tiled=True)  10.6 us
    ppermute x1, starting transfers between devices, across_y(): return lax.ppermute(array, 'row', [(i, (i + 8) % 16) for i in range(16)])  7.73 us
    ppermute x3, waiting for transfers between devices, along_x(): return lax.ppermute(array, 'row', pairs)  7.67 us
    all_to_all x1, waiting for transfers between devices, on_device(): row_back = lax.all_to_all(row_out, 'col', 0, 0, tiled=True)  6.53 us
    all_to_all x1, starting transfers between devices, on_device(): lax.all_to_all(column_out, 'row', 0, 0, tiled=True, axis_index_groups=SAM...  6.41 us
    ppermute x3, starting transfers between devices, across_core(): lax.ppermute(array, 'row', [(i, i // 2 * 2 + (i + 1) % 2) for i in range(...  6.25 us
  transfers between devices with their start and end apart: 11, of which 4 were waited for; matrix products, arithmetic and copies ran while one was open for 0% of the time, Pallas kernels for 9%

profile of v4, /device:TPU:8, one launch (start us, length us, event | category | flops | bytes accessed | tf_op | source)
XLA Modules:
  0.0 85.2 jit_solution(2958114625716701512)
XLA Ops:
  0.0 2.6 %pack.1 = (bf16[56,32,128]{2,1,0:T(8,128)(2,1)S(1)}, bf16[40,32,128]{2,1,0:T(8,128)(2,1)S(1)}, bf16[4,8,10,8,128]{4,3,2,1,0:T(8,128)(2,1)}) custom-call(bf16[6,32,1024]{2,1,0:T(8,128)(2,1)} %bitcast.7, bf16[6,32,1024]{2,1,0:T(8,128)(2,1)} %bitcast.8, bf16[6,32,1024]{2,1,0:T(8,128)(2,1)} %bitcast.9, s32[6,32]{1,0:T(8,128)} %bitcast.11, bf16[64,1024]{1,0:T(8,128)(2,1)} %bitcast.10), custom_call_target="tpu_custom_call" | custom-call | tf_op jit(solution)/shard_map/pack/pallas_call | solution.py:313
  2.6 7.7 %collective-permute-start = (bf16[56,32,128]{2,1,0:T(8,128)(2,1)S(1)}, bf16[56,32,128]{2,1,0:T(8,128)(2,1)S(1)}, u32[]{:S(2)}, u32[]{:S(2)}) collective-permute-start(bf16[56,32,128]{2,1,0:T(8,128)(2,1)S(1)} %get-tuple-element.14.sent_ref), channel_id=1, source_target_pairs={{0,256},{32,288},{64,320},{96,352},{128,384},{160,416},{192,448},{... | collective-permute-start | bytes 1376264 | tf_op jit(solution)/shard_map/ppermute | solution.py:287
  10.3 10.6 %all-to-all-start.1 = ((bf16[32,10,8,128]{3,2,1,0:T(8,128)(2,1)}), bf16[32,10,8,128]{3,2,1,0:T(8,128)(2,1)S(1)}, u32[]{:S(2)}, u32[]{:S(2)}) async-start(bf16[32,10,8,128]{3,2,1,0:T(8,128)(2,1)} %bitcast.5), calls=%async_computation.1 | async-start | bytes 1310720 | tf_op jit(solution)/shard_map/all_to_all | solution.py:324
  21.0 0.1 gather_x.1
  21.1 3.4 %collective-permute-start.1 = (bf16[51,32,128]{2,1,0:T(8,128)(2,1)S(1)}, bf16[51,32,128]{2,1,0:T(8,128)(2,1)S(1)}, u32[]{:S(2)}, u32[]{:S(2)}) collective-permute-start(bf16[51,32,128]{2,1,0:T(8,128)(2,1)S(1)} %get-tuple-element.17), channel_id=1, source_target_pairs={{0,64},{32,96},{64,128},{96,160},{128,192},{160,224},{192,0},{224,... | collective-permute-start | bytes 1253384 | tf_op jit(solution)/shard_map/ppermute | solution.py:296
  24.5 3.7 %collective-permute-start.3 = (bf16[51,32,128]{2,1,0:T(8,128)(2,1)S(1)}, bf16[51,32,128]{2,1,0:T(8,128)(2,1)S(1)}, u32[]{:S(2)}, u32[]{:S(2)}) collective-permute-start(bf16[51,32,128]{2,1,0:T(8,128)(2,1)S(1)} %get-tuple-element.19), channel_id=1, source_target_pairs={{0,192},{32,224},{64,0},{96,32},{128,64},{160,96},{192,128},{224,1... | collective-permute-start | bytes 1253384 | tf_op jit(solution)/shard_map/ppermute | solution.py:296
  28.2 3.7 %collective-permute-start.2 = (bf16[19,32,128]{2,1,0:T(8,128)(2,1)S(1)}, bf16[19,32,128]{2,1,0:T(8,128)(2,1)S(1)}, u32[]{:S(2)}, u32[]{:S(2)}) collective-permute-start(bf16[19,32,128]{2,1,0:T(8,128)(2,1)S(1)} %get-tuple-element.18), channel_id=1, source_target_pairs={{0,128},{32,160},{64,192},{96,224},{128,0},{160,32},{192,64},{224,... | collective-permute-start | bytes 466952 | tf_op jit(solution)/shard_map/ppermute | solution.py:296
  31.9 7.4 %collective-permute-done.2.refs_2_ = bf16[19,32,128]{2,1,0:T(8,128)(2,1)S(1)} collective-permute-done((bf16[19,32,128]{2,1,0:T(8,128)(2,1)S(1)}, bf16[19,32,128]{2,1,0:T(8,128)(2,1)S(1)}, u32[]{:S(2)}, u32[]{:S(2)}) %collective-permute-start.2) | collective-permute-done | bytes 155680 | tf_op jit(solution)/shard_map/ppermute | solution.py:296
  39.3 0.2 collective-permute-done.3.refs_3_.right_ref
  39.6 1.9 %collective-permute-start.4 = (bf16[52,32,128]{2,1,0:T(8,128)(2,1)S(1)}, bf16[52,32,128]{2,1,0:T(8,128)(2,1)S(1)}, u32[]{:S(2)}, u32[]{:S(2)}) collective-permute-start(bf16[52,32,128]{2,1,0:T(8,128)(2,1)S(1)} %stack_keys.1), channel_id=1, source_target_pairs={{0,32},{32,0},{64,96},{96,64},{128,160},{160,128},{192,224},{224,1... | collective-permute-start | bytes 1277960 | tf_op jit(solution)/shard_map/ppermute | solution.py:291
  41.5 0.1 early_weights.1
  41.6 2.4 %collective-permute-start.5 = (bf16[96,32,128]{2,1,0:T(8,128)(2,1)S(1)}, bf16[96,32,128]{2,1,0:T(8,128)(2,1)}, u32[]{:S(2)}, u32[]{:S(2)}) collective-permute-start(bf16[96,32,128]{2,1,0:T(8,128)(2,1)S(1)} %get-tuple-element.21.early_ref), channel_id=1, source_target_pairs={{0,32},{32,0},{64,96},{96,64},{128,160},{160,128},{192,224},{224,1... | collective-permute-start | bytes 2359304 | tf_op jit(solution)/shard_map/ppermute | solution.py:291
  44.0 2.3 %attend_columns.1.after_ref = bf16[8,3,32,128]{3,2,1,0:T(8,128)(2,1)} custom-call(bf16[19,32,128]{2,1,0:T(8,128)(2,1)S(1)} %get-tuple-element.16.refs_0_, bf16[51,32,128]{2,1,0:T(8,128)(2,1)S(1)} %collective-permute-done.1.refs_1_.left_ref, bf16[19,32,128]{2,1,0:T(8,128)(2,1)S(1)} %collective-permute-done.2.refs_2_, ...), custom_call_target="tpu_custom_call" | custom-call | tf_op jit(solution)/shard_map/attend_columns/pallas_call | solution.py:343
  46.4 6.4 %all-to-all-start = ((bf16[8,3,32,128]{3,2,1,0:T(8,128)(2,1)}), bf16[8,3,32,128]{3,2,1,0:T(8,128)(2,1)S(1)}, u32[]{:S(2)}, u32[]{:S(2)}) async-start(bf16[8,3,32,128]{3,2,1,0:T(8,128)(2,1)} %attend_columns.1.after_ref), calls=%async_computation | async-start | bytes 393216 | tf_op jit(solution)/shard_map/all_to_all | solution.py:352
  52.8 3.4 %collective-permute-start.6 = (bf16[32,32,128]{2,1,0:T(8,128)(2,1)S(1)}, bf16[32,32,128]{2,1,0:T(8,128)(2,1)S(1)}, u32[]{:S(2)}, u32[]{:S(2)}) collective-permute-start(bf16[32,32,128]{2,1,0:T(8,128)(2,1)S(1)} %get-tuple-element.22), channel_id=1, source_target_pairs={{0,64},{32,96},{64,0},{96,32},{128,192},{160,224},{192,128},{224,1... | collective-permute-start | bytes 786440 | tf_op jit(solution)/shard_map/ppermute | solution.py:300
  56.1 2.9 %attend_rows.1 = bf16[32,3,8,128]{3,2,1,0:T(8,128)(2,1)} custom-call(bf16[32,10,8,128]{3,2,1,0:T(8,128)(2,1)S(1)} %all-to-all-done.1.in_ref, bf16[8,3,32,128]{3,2,1,0:T(8,128)(2,1)} %attend_columns.1.after_ref), custom_call_target="tpu_custom_call" | custom-call | tf_op jit(solution)/shard_map/attend_rows/pallas_call | solution.py:355
  59.0 12.0 %all-to-all-start.2 = ((bf16[32,3,8,128]{3,2,1,0:T(8,128)(2,1)}), bf16[32,3,8,128]{3,2,1,0:T(8,128)(2,1)S(1)}, u32[]{:S(2)}, u32[]{:S(2)}) async-start(bf16[32,3,8,128]{3,2,1,0:T(8,128)(2,1)} %attend_rows.1), calls=%async_computation.2 | async-start | bytes 393216 | tf_op jit(solution)/shard_map/all_to_all | solution.py:373
  71.0 0.0 copy-start.1
  71.0 1.9 %collective-permute-start.7 = (bf16[32,32,128]{2,1,0:T(8,128)(2,1)S(1)}, bf16[32,32,128]{2,1,0:T(8,128)(2,1)S(1)}, u32[]{:S(2)}, u32[]{:S(2)}) collective-permute-start(bf16[32,32,128]{2,1,0:T(8,128)(2,1)S(1)} %collective-permute-done.6.late_ref), channel_id=1, source_target_pairs={{0,32},{32,0},{64,96},{96,64},{128,160},{160,128},{192,224},{224,1... | collective-permute-start | bytes 786440 | tf_op jit(solution)/shard_map/ppermute | solution.py:291
  73.0 1.5 %collective-permute-done.7.late_other_ref = bf16[32,32,128]{2,1,0:T(8,128)(2,1)S(1)} collective-permute-done((bf16[32,32,128]{2,1,0:T(8,128)(2,1)S(1)}, bf16[32,32,128]{2,1,0:T(8,128)(2,1)S(1)}, u32[]{:S(2)}, u32[]{:S(2)}) %collective-permute-start.7) | collective-permute-done | bytes 262176 | tf_op jit(solution)/shard_map/ppermute | solution.py:291
  74.5 0.7 copy-done.2
  75.2 1.9 %assemble_weights.1.w_ref = bf16[1024,1024]{1,0:T(8,128)(2,1)S(1)} custom-call(bf16[96,32,128]{2,1,0:T(8,128)(2,1)} %copy-done, bf16[96,32,128]{2,1,0:T(8,128)(2,1)} %collective-permute-done.5.early_other_ref, bf16[32,32,128]{2,1,0:T(8,128)(2,1)} %copy-done.1, bf16[32,32,128]{2,1,0:T(8,128)(2,1)} %copy-done.2), custom_call_target="tpu_custom_call" | custom-call | tf_op jit(solution)/shard_map/assemble_weights/pallas_call | solution.py:370
  77.1 6.5 %all-to-all-done.2.row_ref = bf16[32,3,8,128]{3,2,1,0:T(8,128)(2,1)S(1)} async-done(((bf16[32,3,8,128]{3,2,1,0:T(8,128)(2,1)}), bf16[32,3,8,128]{3,2,1,0:T(8,128)(2,1)S(1)}, u32[]{:S(2)}, u32[]{:S(2)}) %all-to-all-start.2) | async-done | bytes 196640 | tf_op jit(solution)/shard_map/all_to_all | solution.py:373
  83.6 1.6 %project.1 = bf16[6,32,1024]{2,1,0:T(8,128)(2,1)} custom-call(bf16[8,3,32,128]{3,2,1,0:T(8,128)(2,1)S(1)} %all-to-all-done.column_ref, bf16[32,3,8,128]{3,2,1,0:T(8,128)(2,1)S(1)} %all-to-all-done.2.row_ref, bf16[1024,1024]{1,0:T(8,128)(2,1)S(1)} %assemble_weights.1.w_ref), custom_call_target="tpu_custom_call" | custom-call | tf_op jit(solution)/shard_map/project/pallas_call | solution.py:374
  (12 shorter events, 0.1 us)
Async XLA Ops:
  2.6 18.4 %collective-permute-start = (bf16[56,32,128]{2,1,0:T(8,128)(2,1)S(1)}, bf16[56,32,128]{2,1,0:T(8,128)(2,1)S(1)}, u32[]{:S(2)}, u32[]{:S(2)}) collective-permute-start(bf16[56,32,128]{2,1,0:T(8,128)(2,1)S(1)} %get-tuple-element.14.sent_ref), channel_id=1, source_target_pairs={{0,256},{32,288},{64,320},{96,352},{128,384},{160,416},{192,448},{... | collective-permute-start | bytes 1376264 | tf_op jit(solution)/shard_map/ppermute | solution.py:287
  10.3 36.0 %all-to-all-start.1 = ((bf16[32,10,8,128]{3,2,1,0:T(8,128)(2,1)}), bf16[32,10,8,128]{3,2,1,0:T(8,128)(2,1)S(1)}, u32[]{:S(2)}, u32[]{:S(2)}) async-start(bf16[32,10,8,128]{3,2,1,0:T(8,128)(2,1)} %bitcast.5), calls=%async_computation.1 | async-start | bytes 1310720 | tf_op jit(solution)/shard_map/all_to_all | solution.py:324
  21.1 18.2 %collective-permute-start.1 = (bf16[51,32,128]{2,1,0:T(8,128)(2,1)S(1)}, bf16[51,32,128]{2,1,0:T(8,128)(2,1)S(1)}, u32[]{:S(2)}, u32[]{:S(2)}) collective-permute-start(bf16[51,32,128]{2,1,0:T(8,128)(2,1)S(1)} %get-tuple-element.17), channel_id=1, source_target_pairs={{0,64},{32,96},{64,128},{96,160},{128,192},{160,224},{192,0},{224,... | collective-permute-start | bytes 1253384 | tf_op jit(solution)/shard_map/ppermute | solution.py:296
  24.5 15.1 %collective-permute-start.3 = (bf16[51,32,128]{2,1,0:T(8,128)(2,1)S(1)}, bf16[51,32,128]{2,1,0:T(8,128)(2,1)S(1)}, u32[]{:S(2)}, u32[]{:S(2)}) collective-permute-start(bf16[51,32,128]{2,1,0:T(8,128)(2,1)S(1)} %get-tuple-element.19), channel_id=1, source_target_pairs={{0,192},{32,224},{64,0},{96,32},{128,64},{160,96},{192,128},{224,1... | collective-permute-start | bytes 1253384 | tf_op jit(solution)/shard_map/ppermute | solution.py:296
  28.2 11.2 %collective-permute-start.2 = (bf16[19,32,128]{2,1,0:T(8,128)(2,1)S(1)}, bf16[19,32,128]{2,1,0:T(8,128)(2,1)S(1)}, u32[]{:S(2)}, u32[]{:S(2)}) collective-permute-start(bf16[19,32,128]{2,1,0:T(8,128)(2,1)S(1)} %get-tuple-element.18), channel_id=1, source_target_pairs={{0,128},{32,160},{64,192},{96,224},{128,0},{160,32},{192,64},{224,... | collective-permute-start | bytes 466952 | tf_op jit(solution)/shard_map/ppermute | solution.py:296
  39.6 4.4 %collective-permute-start.4 = (bf16[52,32,128]{2,1,0:T(8,128)(2,1)S(1)}, bf16[52,32,128]{2,1,0:T(8,128)(2,1)S(1)}, u32[]{:S(2)}, u32[]{:S(2)}) collective-permute-start(bf16[52,32,128]{2,1,0:T(8,128)(2,1)S(1)} %stack_keys.1), channel_id=1, source_target_pairs={{0,32},{32,0},{64,96},{96,64},{128,160},{160,128},{192,224},{224,1... | collective-permute-start | bytes 1277960 | tf_op jit(solution)/shard_map/ppermute | solution.py:291
  41.6 32.9 %copy-start = (bf16[96,32,128]{2,1,0:T(8,128)(2,1)}, bf16[96,32,128]{2,1,0:T(8,128)(2,1)S(1)}, u32[]{:S(2)}) copy-start(bf16[96,32,128]{2,1,0:T(8,128)(2,1)S(1)} %get-tuple-element.21.early_ref) | copy-start | bytes 2359300
  41.6 32.9 %collective-permute-start.5 = (bf16[96,32,128]{2,1,0:T(8,128)(2,1)S(1)}, bf16[96,32,128]{2,1,0:T(8,128)(2,1)}, u32[]{:S(2)}, u32[]{:S(2)}) collective-permute-start(bf16[96,32,128]{2,1,0:T(8,128)(2,1)S(1)} %get-tuple-element.21.early_ref), channel_id=1, source_target_pairs={{0,32},{32,0},{64,96},{96,64},{128,160},{160,128},{192,224},{224,1... | collective-permute-start | bytes 2359304 | tf_op jit(solution)/shard_map/ppermute | solution.py:291
  46.4 12.7 %all-to-all-start = ((bf16[8,3,32,128]{3,2,1,0:T(8,128)(2,1)}), bf16[8,3,32,128]{3,2,1,0:T(8,128)(2,1)S(1)}, u32[]{:S(2)}, u32[]{:S(2)}) async-start(bf16[8,3,32,128]{3,2,1,0:T(8,128)(2,1)} %attend_columns.1.after_ref), calls=%async_computation | async-start | bytes 393216 | tf_op jit(solution)/shard_map/all_to_all | solution.py:352
  52.8 18.2 %collective-permute-start.6 = (bf16[32,32,128]{2,1,0:T(8,128)(2,1)S(1)}, bf16[32,32,128]{2,1,0:T(8,128)(2,1)S(1)}, u32[]{:S(2)}, u32[]{:S(2)}) collective-permute-start(bf16[32,32,128]{2,1,0:T(8,128)(2,1)S(1)} %get-tuple-element.22), channel_id=1, source_target_pairs={{0,64},{32,96},{64,0},{96,32},{128,192},{160,224},{192,128},{224,1... | collective-permute-start | bytes 786440 | tf_op jit(solution)/shard_map/ppermute | solution.py:300
  59.0 24.6 %all-to-all-start.2 = ((bf16[32,3,8,128]{3,2,1,0:T(8,128)(2,1)}), bf16[32,3,8,128]{3,2,1,0:T(8,128)(2,1)S(1)}, u32[]{:S(2)}, u32[]{:S(2)}) async-start(bf16[32,3,8,128]{3,2,1,0:T(8,128)(2,1)} %attend_rows.1), calls=%async_computation.2 | async-start | bytes 393216 | tf_op jit(solution)/shard_map/all_to_all | solution.py:373
  71.0 3.4 %copy-start.1 = (bf16[32,32,128]{2,1,0:T(8,128)(2,1)}, bf16[32,32,128]{2,1,0:T(8,128)(2,1)S(1)}, u32[]{:S(2)}) copy-start(bf16[32,32,128]{2,1,0:T(8,128)(2,1)S(1)} %collective-permute-done.6.late_ref) | copy-start | bytes 786436
  71.0 3.4 %collective-permute-start.7 = (bf16[32,32,128]{2,1,0:T(8,128)(2,1)S(1)}, bf16[32,32,128]{2,1,0:T(8,128)(2,1)S(1)}, u32[]{:S(2)}, u32[]{:S(2)}) collective-permute-start(bf16[32,32,128]{2,1,0:T(8,128)(2,1)S(1)} %collective-permute-done.6.late_ref), channel_id=1, source_target_pairs={{0,32},{32,0},{64,96},{96,64},{128,160},{160,128},{192,224},{224,1... | collective-permute-start | bytes 786440 | tf_op jit(solution)/shard_map/ppermute | solution.py:291
  74.5 0.7 copy-start.2

commit v5 on v4

--- a/solution.py
+++ b/solution.py
@@ -57,8 +57,7 @@
     return me // 8, (me // 2) % 4, me % 2
 
 
-def pack_rows(q_ref, k_ref, v_ref, m_ref, out_ref, out_hbm, sems):
-    outgoing = []
+def pack_rows(q_ref, k_ref, v_ref, m_ref, out_ref):
     bias = bias_lanes(m_ref[...], 0, 0, 6)
     low = low_lanes((6, 32, 128))
     for pair in range(HALF // 2):
@@ -80,13 +79,10 @@
                 out_ref[rg, h, 0:6] = qk[:, rows].astype(jnp.bfloat16)
                 out_ref[rg, h, 6:9] = vv[:, rows].astype(jnp.bfloat16)
                 out_ref[rg, h, 9] = bias[rows].astype(jnp.bfloat16)
-        heads = pl.ds(2 * pair, 2)
-        outgoing += start([(out_ref.at[:, heads], out_hbm.at[:, heads])], sems, pair)
-    return outgoing
-
-
-def pack_kernel(q_hbm, k_hbm, v_hbm, m_hbm, w_hbm, send_ref, keep_ref, out_hbm, *refs):
-    (*row_refs, m_ref, sems, out_ref, out_sems), (y, _, _) = refs, place()
+
+
+def pack_kernel(q_hbm, k_hbm, v_hbm, m_hbm, w_hbm, send_ref, keep_ref, out_ref, *refs):
+    (*row_refs, m_ref, sems), (y, _, _) = refs, place()
     copies = [(m_hbm, m_ref)]
     for source, target in zip((q_hbm, k_hbm, v_hbm), row_refs):
         copies.append((source.at[:, :, pl.ds(WIDTH, WIDTH)], target))
@@ -102,13 +98,12 @@
         copies.append((w_hbm.at[rows, lanes], send_ref.at[4 * UNIT + n]))
     copies = start(copies, sems)
     wait(copies[:4])
-    outgoing = pack_rows(*row_refs, m_ref, out_ref, out_hbm, out_sems)
+    pack_rows(*row_refs, m_ref, out_ref)
     wait(copies[4:])
     for ref, half in ((send_ref, 1 - y), (keep_ref, y)):
         bias = bias_lanes(m_ref[...], 3 * half, 0, 3).astype(jnp.bfloat16)
         for pair in range(4):
             ref[UNIT * pair + UNIT - 1] = bias
-    wait(outgoing)
 
 
 def shift_lanes(tile, shift):
@@ -173,7 +168,7 @@
     return summed / totals
 
 
-def attend_rows_kernel(in_ref, after_ref, out_hbm, qk_ref, v_ref, b_ref, o_ref, out_ref, sems):
+def attend_rows_kernel(in_ref, after_ref, out_ref, qk_ref, v_ref, b_ref, o_ref):
     for t in range(6):
         qk_ref[t * 256 : t * 256 + 256] = (
             in_ref[:, t].astype(jnp.float32).reshape(256, 128)
@@ -192,13 +187,10 @@
         out = attend(qk[:, :HEAD], qk[:, HEAD:], v, bias)
         out = out.T
         o_ref[pl.ds(r, 96, stride=8), :] = jnp.concatenate([out[:96], out[96:]], axis=1)
-    outgoing = []
     for j in range(3):
         out_ref[:, j] = (
             o_ref[j * 256 : j * 256 + 256].reshape(32, 8, 128).astype(jnp.bfloat16)
         )
-        outgoing += start([(out_ref.at[:, j], out_hbm.at[:, j])], sems, j)
-    wait(outgoing)
 
 
 def attend_columns_kernel(*refs):
@@ -316,9 +308,7 @@
         "pack",
         [hbm] * 5,
         [pltpu.VMEM((6, 32, WIDTH), jnp.bfloat16)] * 3
-        + [pltpu.VMEM((6, 32), jnp.int32), pltpu.SemaphoreType.DMA((44,))]
-        + [pltpu.VMEM((4, 8, 10, 8, 128), jnp.bfloat16), pltpu.SemaphoreType.DMA((4,))],
-        [vmem, vmem, hbm],
+        + [pltpu.VMEM((6, 32), jnp.int32), pltpu.SemaphoreType.DMA((44,))],
     )(*tokens, merges, w_part)
     other = across_y(sent)
     row_moved = lax.all_to_all(row_packed.reshape(32, 10, 8, 128), "col", 0, 0, tiled=True)
@@ -362,10 +352,7 @@
             pltpu.VMEM((768, 128), jnp.float32),
             pltpu.VMEM((256, 128), jnp.float32),
             pltpu.VMEM((768, 128), jnp.float32),
-            pltpu.VMEM((32, 3, 8, 128), jnp.bfloat16),
-            pltpu.SemaphoreType.DMA((3,)),
         ],
-        [hbm],
     )(row_moved, column_done)
     (weights,) = call(
         assemble_weights_kernel, [(2 * WIDTH, 2 * WIDTH)], "assemble_weights", [vmem] * 4

time: 85.8 us -> 85.8 us (level)
  no operation moved by 1% of the time
where the time goes in v5:
time: 85.8 us; the launch traced here: 85.2 us
  starting transfers between devices  57.1 us (67%)
  waiting for transfers between devices  15.7 us (18%)
  Pallas kernels  11.5 us (13%)
    all_to_all x1, starting transfers between devices, on_device(): row_back = lax.all_to_all(row_out, 'col', 0, 0, tiled=True)  11.9 us
    ppermute x3, starting transfers between devices, along_x(): return lax.ppermute(array, 'row', pairs)  10.8 us
    all_to_all x1, starting transfers between devices, on_device(): lax.all_to_all(row_packed.reshape(32, 10, 8, 128), 'col', 0, 0, tiled=True)  10.6 us
    ppermute x1, starting transfers between devices, across_y(): return lax.ppermute(array, 'row', [(i, (i + 8) % 16) for i in range(16)])  7.73 us
    ppermute x3, waiting for transfers between devices, along_x(): return lax.ppermute(array, 'row', pairs)  7.67 us
    all_to_all x1, waiting for transfers between devices, on_device(): row_back = lax.all_to_all(row_out, 'col', 0, 0, tiled=True)  6.54 us
    all_to_all x1, starting transfers between devices, on_device(): lax.all_to_all(column_out, 'row', 0, 0, tiled=True, axis_index_groups=SAM...  6.41 us
    ppermute x3, starting transfers between devices, across_core(): lax.ppermute(array, 'row', [(i, i // 2 * 2 + (i + 1) % 2) for i in range(...  6.25 us
  transfers between devices with their start and end apart: 11, of which 4 were waited for; matrix products, arithmetic and copies ran while one was open for 0% of the time, Pallas kernels for 9%

profile of v5, /device:TPU:8, one launch (start us, length us, event | category | flops | bytes accessed | tf_op | source)
XLA Modules:
  0.0 85.2 jit_solution(6504320120304090563)
XLA Ops:
  0.0 2.7 %pack.1 = (bf16[56,32,128]{2,1,0:T(8,128)(2,1)S(1)}, bf16[40,32,128]{2,1,0:T(8,128)(2,1)S(1)}, bf16[4,8,10,8,128]{4,3,2,1,0:T(8,128)(2,1)}) custom-call(bf16[6,32,1024]{2,1,0:T(8,128)(2,1)} %bitcast.7, bf16[6,32,1024]{2,1,0:T(8,128)(2,1)} %bitcast.8, bf16[6,32,1024]{2,1,0:T(8,128)(2,1)} %bitcast.9, s32[6,32]{1,0:T(8,128)} %bitcast.11, bf16[64,1024]{1,0:T(8,128)(2,1)} %bitcast.10), custom_call_target="tpu_custom_call" | custom-call | tf_op jit(solution)/shard_map/pack/pallas_call | solution.py:305
  2.7 7.7 %collective-permute-start = (bf16[56,32,128]{2,1,0:T(8,128)(2,1)S(1)}, bf16[56,32,128]{2,1,0:T(8,128)(2,1)S(1)}, u32[]{:S(2)}, u32[]{:S(2)}) collective-permute-start(bf16[56,32,128]{2,1,0:T(8,128)(2,1)S(1)} %get-tuple-element.14.sent_ref), channel_id=1, source_target_pairs={{0,256},{32,288},{64,320},{96,352},{128,384},{160,416},{192,448},{... | collective-permute-start | bytes 1376264 | tf_op jit(solution)/shard_map/ppermute | solution.py:279
  10.4 10.6 %all-to-all-start.1 = ((bf16[32,10,8,128]{3,2,1,0:T(8,128)(2,1)}), bf16[32,10,8,128]{3,2,1,0:T(8,128)(2,1)S(1)}, u32[]{:S(2)}, u32[]{:S(2)}) async-start(bf16[32,10,8,128]{3,2,1,0:T(8,128)(2,1)} %bitcast.5), calls=%async_computation.1 | async-start | bytes 1310720 | tf_op jit(solution)/shard_map/all_to_all | solution.py:314
  21.0 0.1 gather_x.1
  21.2 3.4 %collective-permute-start.1 = (bf16[51,32,128]{2,1,0:T(8,128)(2,1)S(1)}, bf16[51,32,128]{2,1,0:T(8,128)(2,1)S(1)}, u32[]{:S(2)}, u32[]{:S(2)}) collective-permute-start(bf16[51,32,128]{2,1,0:T(8,128)(2,1)S(1)} %get-tuple-element.17), channel_id=1, source_target_pairs={{0,64},{32,96},{64,128},{96,160},{128,192},{160,224},{192,0},{224,... | collective-permute-start | bytes 1253384 | tf_op jit(solution)/shard_map/ppermute | solution.py:288
  24.6 3.7 %collective-permute-start.3 = (bf16[51,32,128]{2,1,0:T(8,128)(2,1)S(1)}, bf16[51,32,128]{2,1,0:T(8,128)(2,1)S(1)}, u32[]{:S(2)}, u32[]{:S(2)}) collective-permute-start(bf16[51,32,128]{2,1,0:T(8,128)(2,1)S(1)} %get-tuple-element.19), channel_id=1, source_target_pairs={{0,192},{32,224},{64,0},{96,32},{128,64},{160,96},{192,128},{224,1... | collective-permute-start | bytes 1253384 | tf_op jit(solution)/shard_map/ppermute | solution.py:288
  28.2 3.7 %collective-permute-start.2 = (bf16[19,32,128]{2,1,0:T(8,128)(2,1)S(1)}, bf16[19,32,128]{2,1,0:T(8,128)(2,1)S(1)}, u32[]{:S(2)}, u32[]{:S(2)}) collective-permute-start(bf16[19,32,128]{2,1,0:T(8,128)(2,1)S(1)} %get-tuple-element.18), channel_id=1, source_target_pairs={{0,128},{32,160},{64,192},{96,224},{128,0},{160,32},{192,64},{224,... | collective-permute-start | bytes 466952 | tf_op jit(solution)/shard_map/ppermute | solution.py:288
  31.9 7.4 %collective-permute-done.2.refs_2_ = bf16[19,32,128]{2,1,0:T(8,128)(2,1)S(1)} collective-permute-done((bf16[19,32,128]{2,1,0:T(8,128)(2,1)S(1)}, bf16[19,32,128]{2,1,0:T(8,128)(2,1)S(1)}, u32[]{:S(2)}, u32[]{:S(2)}) %collective-permute-start.2) | collective-permute-done | bytes 155680 | tf_op jit(solution)/shard_map/ppermute | solution.py:288
  39.4 0.2 collective-permute-done.3.refs_3_.right_ref
  39.7 1.9 %collective-permute-start.4 = (bf16[52,32,128]{2,1,0:T(8,128)(2,1)S(1)}, bf16[52,32,128]{2,1,0:T(8,128)(2,1)S(1)}, u32[]{:S(2)}, u32[]{:S(2)}) collective-permute-start(bf16[52,32,128]{2,1,0:T(8,128)(2,1)S(1)} %stack_keys.1), channel_id=1, source_target_pairs={{0,32},{32,0},{64,96},{96,64},{128,160},{160,128},{192,224},{224,1... | collective-permute-start | bytes 1277960 | tf_op jit(solution)/shard_map/ppermute | solution.py:283
  41.6 0.1 early_weights.1
  41.7 2.4 %collective-permute-start.5 = (bf16[96,32,128]{2,1,0:T(8,128)(2,1)S(1)}, bf16[96,32,128]{2,1,0:T(8,128)(2,1)}, u32[]{:S(2)}, u32[]{:S(2)}) collective-permute-start(bf16[96,32,128]{2,1,0:T(8,128)(2,1)S(1)} %get-tuple-element.21.early_ref), channel_id=1, source_target_pairs={{0,32},{32,0},{64,96},{96,64},{128,160},{160,128},{192,224},{224,1... | collective-permute-start | bytes 2359304 | tf_op jit(solution)/shard_map/ppermute | solution.py:283
  44.1 2.3 %attend_columns.1.after_ref = bf16[8,3,32,128]{3,2,1,0:T(8,128)(2,1)} custom-call(bf16[19,32,128]{2,1,0:T(8,128)(2,1)S(1)} %get-tuple-element.16.refs_0_, bf16[51,32,128]{2,1,0:T(8,128)(2,1)S(1)} %collective-permute-done.1.refs_1_.left_ref, bf16[19,32,128]{2,1,0:T(8,128)(2,1)S(1)} %collective-permute-done.2.refs_2_, ...), custom_call_target="tpu_custom_call" | custom-call | tf_op jit(solution)/shard_map/attend_columns/pallas_call | solution.py:333
  46.4 6.4 %all-to-all-start = ((bf16[8,3,32,128]{3,2,1,0:T(8,128)(2,1)}), bf16[8,3,32,128]{3,2,1,0:T(8,128)(2,1)S(1)}, u32[]{:S(2)}, u32[]{:S(2)}) async-start(bf16[8,3,32,128]{3,2,1,0:T(8,128)(2,1)} %attend_columns.1.after_ref), calls=%async_computation | async-start | bytes 393216 | tf_op jit(solution)/shard_map/all_to_all | solution.py:342
  52.8 3.4 %collective-permute-start.6 = (bf16[32,32,128]{2,1,0:T(8,128)(2,1)S(1)}, bf16[32,32,128]{2,1,0:T(8,128)(2,1)S(1)}, u32[]{:S(2)}, u32[]{:S(2)}) collective-permute-start(bf16[32,32,128]{2,1,0:T(8,128)(2,1)S(1)} %get-tuple-element.22), channel_id=1, source_target_pairs={{0,64},{32,96},{64,0},{96,32},{128,192},{160,224},{192,128},{224,1... | collective-permute-start | bytes 786440 | tf_op jit(solution)/shard_map/ppermute | solution.py:292
  56.2 2.8 %attend_rows.1 = bf16[32,3,8,128]{3,2,1,0:T(8,128)(2,1)} custom-call(bf16[32,10,8,128]{3,2,1,0:T(8,128)(2,1)S(1)} %all-to-all-done.1.in_ref, bf16[8,3,32,128]{3,2,1,0:T(8,128)(2,1)} %attend_columns.1.after_ref), custom_call_target="tpu_custom_call" | custom-call | tf_op jit(solution)/shard_map/attend_rows/pallas_call | solution.py:345
  59.0 11.9 %all-to-all-start.2 = ((bf16[32,3,8,128]{3,2,1,0:T(8,128)(2,1)}), bf16[32,3,8,128]{3,2,1,0:T(8,128)(2,1)S(1)}, u32[]{:S(2)}, u32[]{:S(2)}) async-start(bf16[32,3,8,128]{3,2,1,0:T(8,128)(2,1)} %attend_rows.1), calls=%async_computation.2 | async-start | bytes 393216 | tf_op jit(solution)/shard_map/all_to_all | solution.py:360
  71.0 0.0 copy-start.1
  71.0 1.9 %collective-permute-start.7 = (bf16[32,32,128]{2,1,0:T(8,128)(2,1)S(1)}, bf16[32,32,128]{2,1,0:T(8,128)(2,1)S(1)}, u32[]{:S(2)}, u32[]{:S(2)}) collective-permute-start(bf16[32,32,128]{2,1,0:T(8,128)(2,1)S(1)} %collective-permute-done.6.late_ref), channel_id=1, source_target_pairs={{0,32},{32,0},{64,96},{96,64},{128,160},{160,128},{192,224},{224,1... | collective-permute-start | bytes 786440 | tf_op jit(solution)/shard_map/ppermute | solution.py:283
  73.0 1.5 %collective-permute-done.7.late_other_ref = bf16[32,32,128]{2,1,0:T(8,128)(2,1)S(1)} collective-permute-done((bf16[32,32,128]{2,1,0:T(8,128)(2,1)S(1)}, bf16[32,32,128]{2,1,0:T(8,128)(2,1)S(1)}, u32[]{:S(2)}, u32[]{:S(2)}) %collective-permute-start.7) | collective-permute-done | bytes 262176 | tf_op jit(solution)/shard_map/ppermute | solution.py:283
  74.5 0.7 copy-done.2
  75.2 1.9 %assemble_weights.1.w_ref = bf16[1024,1024]{1,0:T(8,128)(2,1)S(1)} custom-call(bf16[96,32,128]{2,1,0:T(8,128)(2,1)} %copy-done, bf16[96,32,128]{2,1,0:T(8,128)(2,1)} %collective-permute-done.5.early_other_ref, bf16[32,32,128]{2,1,0:T(8,128)(2,1)} %copy-done.1, bf16[32,32,128]{2,1,0:T(8,128)(2,1)} %copy-done.2), custom_call_target="tpu_custom_call" | custom-call | tf_op jit(solution)/shard_map/assemble_weights/pallas_call | solution.py:357
  77.1 6.5 %all-to-all-done.2.row_ref = bf16[32,3,8,128]{3,2,1,0:T(8,128)(2,1)S(1)} async-done(((bf16[32,3,8,128]{3,2,1,0:T(8,128)(2,1)}), bf16[32,3,8,128]{3,2,1,0:T(8,128)(2,1)S(1)}, u32[]{:S(2)}, u32[]{:S(2)}) %all-to-all-start.2) | async-done | bytes 196640 | tf_op jit(solution)/shard_map/all_to_all | solution.py:360
  83.6 1.6 %project.1 = bf16[6,32,1024]{2,1,0:T(8,128)(2,1)} custom-call(bf16[8,3,32,128]{3,2,1,0:T(8,128)(2,1)S(1)} %all-to-all-done.column_ref, bf16[32,3,8,128]{3,2,1,0:T(8,128)(2,1)S(1)} %all-to-all-done.2.row_ref, bf16[1024,1024]{1,0:T(8,128)(2,1)S(1)} %assemble_weights.1.w_ref), custom_call_target="tpu_custom_call" | custom-call | tf_op jit(solution)/shard_map/project/pallas_call | solution.py:361
  (12 shorter events, 0.1 us)
Async XLA Ops:
  2.7 18.4 %collective-permute-start = (bf16[56,32,128]{2,1,0:T(8,128)(2,1)S(1)}, bf16[56,32,128]{2,1,0:T(8,128)(2,1)S(1)}, u32[]{:S(2)}, u32[]{:S(2)}) collective-permute-start(bf16[56,32,128]{2,1,0:T(8,128)(2,1)S(1)} %get-tuple-element.14.sent_ref), channel_id=1, source_target_pairs={{0,256},{32,288},{64,320},{96,352},{128,384},{160,416},{192,448},{... | collective-permute-start | bytes 1376264 | tf_op jit(solution)/shard_map/ppermute | solution.py:279
  10.4 36.0 %all-to-all-start.1 = ((bf16[32,10,8,128]{3,2,1,0:T(8,128)(2,1)}), bf16[32,10,8,128]{3,2,1,0:T(8,128)(2,1)S(1)}, u32[]{:S(2)}, u32[]{:S(2)}) async-start(bf16[32,10,8,128]{3,2,1,0:T(8,128)(2,1)} %bitcast.5), calls=%async_computation.1 | async-start | bytes 1310720 | tf_op jit(solution)/shard_map/all_to_all | solution.py:314
  21.2 18.2 %collective-permute-start.1 = (bf16[51,32,128]{2,1,0:T(8,128)(2,1)S(1)}, bf16[51,32,128]{2,1,0:T(8,128)(2,1)S(1)}, u32[]{:S(2)}, u32[]{:S(2)}) collective-permute-start(bf16[51,32,128]{2,1,0:T(8,128)(2,1)S(1)} %get-tuple-element.17), channel_id=1, source_target_pairs={{0,64},{32,96},{64,128},{96,160},{128,192},{160,224},{192,0},{224,... | collective-permute-start | bytes 1253384 | tf_op jit(solution)/shard_map/ppermute | solution.py:288
  24.6 15.1 %collective-permute-start.3 = (bf16[51,32,128]{2,1,0:T(8,128)(2,1)S(1)}, bf16[51,32,128]{2,1,0:T(8,128)(2,1)S(1)}, u32[]{:S(2)}, u32[]{:S(2)}) collective-permute-start(bf16[51,32,128]{2,1,0:T(8,128)(2,1)S(1)} %get-tuple-element.19), channel_id=1, source_target_pairs={{0,192},{32,224},{64,0},{96,32},{128,64},{160,96},{192,128},{224,1... | collective-permute-start | bytes 1253384 | tf_op jit(solution)/shard_map/ppermute | solution.py:288
  28.2 11.2 %collective-permute-start.2 = (bf16[19,32,128]{2,1,0:T(8,128)(2,1)S(1)}, bf16[19,32,128]{2,1,0:T(8,128)(2,1)S(1)}, u32[]{:S(2)}, u32[]{:S(2)}) collective-permute-start(bf16[19,32,128]{2,1,0:T(8,128)(2,1)S(1)} %get-tuple-element.18), channel_id=1, source_target_pairs={{0,128},{32,160},{64,192},{96,224},{128,0},{160,32},{192,64},{224,... | collective-permute-start | bytes 466952 | tf_op jit(solution)/shard_map/ppermute | solution.py:288
  39.7 4.4 %collective-permute-start.4 = (bf16[52,32,128]{2,1,0:T(8,128)(2,1)S(1)}, bf16[52,32,128]{2,1,0:T(8,128)(2,1)S(1)}, u32[]{:S(2)}, u32[]{:S(2)}) collective-permute-start(bf16[52,32,128]{2,1,0:T(8,128)(2,1)S(1)} %stack_keys.1), channel_id=1, source_target_pairs={{0,32},{32,0},{64,96},{96,64},{128,160},{160,128},{192,224},{224,1... | collective-permute-start | bytes 1277960 | tf_op jit(solution)/shard_map/ppermute | solution.py:283
  41.7 32.8 %copy-start = (bf16[96,32,128]{2,1,0:T(8,128)(2,1)}, bf16[96,32,128]{2,1,0:T(8,128)(2,1)S(1)}, u32[]{:S(2)}) copy-start(bf16[96,32,128]{2,1,0:T(8,128)(2,1)S(1)} %get-tuple-element.21.early_ref) | copy-start | bytes 2359300
  41.7 32.8 %collective-permute-start.5 = (bf16[96,32,128]{2,1,0:T(8,128)(2,1)S(1)}, bf16[96,32,128]{2,1,0:T(8,128)(2,1)}, u32[]{:S(2)}, u32[]{:S(2)}) collective-permute-start(bf16[96,32,128]{2,1,0:T(8,128)(2,1)S(1)} %get-tuple-element.21.early_ref), channel_id=1, source_target_pairs={{0,32},{32,0},{64,96},{96,64},{128,160},{160,128},{192,224},{224,1... | collective-permute-start | bytes 2359304 | tf_op jit(solution)/shard_map/ppermute | solution.py:283
  46.4 12.6 %all-to-all-start = ((bf16[8,3,32,128]{3,2,1,0:T(8,128)(2,1)}), bf16[8,3,32,128]{3,2,1,0:T(8,128)(2,1)S(1)}, u32[]{:S(2)}, u32[]{:S(2)}) async-start(bf16[8,3,32,128]{3,2,1,0:T(8,128)(2,1)} %attend_columns.1.after_ref), calls=%async_computation | async-start | bytes 393216 | tf_op jit(solution)/shard_map/all_to_all | solution.py:342
  52.8 18.2 %collective-permute-start.6 = (bf16[32,32,128]{2,1,0:T(8,128)(2,1)S(1)}, bf16[32,32,128]{2,1,0:T(8,128)(2,1)S(1)}, u32[]{:S(2)}, u32[]{:S(2)}) collective-permute-start(bf16[32,32,128]{2,1,0:T(8,128)(2,1)S(1)} %get-tuple-element.22), channel_id=1, source_target_pairs={{0,64},{32,96},{64,0},{96,32},{128,192},{160,224},{192,128},{224,1... | collective-permute-start | bytes 786440 | tf_op jit(solution)/shard_map/ppermute | solution.py:292
  59.0 24.6 %all-to-all-start.2 = ((bf16[32,3,8,128]{3,2,1,0:T(8,128)(2,1)}), bf16[32,3,8,128]{3,2,1,0:T(8,128)(2,1)S(1)}, u32[]{:S(2)}, u32[]{:S(2)}) async-start(bf16[32,3,8,128]{3,2,1,0:T(8,128)(2,1)} %attend_rows.1), calls=%async_computation.2 | async-start | bytes 393216 | tf_op jit(solution)/shard_map/all_to_all | solution.py:360
  71.0 3.4 %copy-start.1 = (bf16[32,32,128]{2,1,0:T(8,128)(2,1)}, bf16[32,32,128]{2,1,0:T(8,128)(2,1)S(1)}, u32[]{:S(2)}) copy-start(bf16[32,32,128]{2,1,0:T(8,128)(2,1)S(1)} %collective-permute-done.6.late_ref) | copy-start | bytes 786436
  71.0 3.4 %collective-permute-start.7 = (bf16[32,32,128]{2,1,0:T(8,128)(2,1)S(1)}, bf16[32,32,128]{2,1,0:T(8,128)(2,1)S(1)}, u32[]{:S(2)}, u32[]{:S(2)}) collective-permute-start(bf16[32,32,128]{2,1,0:T(8,128)(2,1)S(1)} %collective-permute-done.6.late_ref), channel_id=1, source_target_pairs={{0,32},{32,0},{64,96},{96,64},{128,160},{160,128},{192,224},{224,1... | collective-permute-start | bytes 786440 | tf_op jit(solution)/shard_map/ppermute | solution.py:283
  74.5 0.7 copy-start.2
